TPU v7x, 256 devices: a whole 4x4x8 slice. The times are simulated.
256 devices in a mesh: seq: 32 (over z, x), tp: 8 (over y, core).
Axes of the slice: x: 4, y: 4, z: 8, core: 2. Of those that a mesh axis runs over, the one named last changes fastest.
Arguments:
- queries: bfloat16 [8192, 4096], P('seq', 'tp'), may hold values from -6 to 6
- keys: bfloat16 [8192, 4096], P('seq', 'tp'), may hold values from -6 to 6
- values: bfloat16 [8192, 4096], P('seq', 'tp'), may hold values from -6 to 6
- log_decay: float32 [32, 8192], P('tp', 'seq'), may hold values from -1 to 0
- residual: bfloat16 [8192, 3072], P('seq', 'tp'), may hold values from -8 to 8
- out_weight: bfloat16 [4096, 3072], P('tp'), may hold values from -0.125 to 0.125
- prenorm_multiplier: float32 [3072], P('tp'), may hold values from 0.25 to 1.75
- router_weight: bfloat16 [3072, 32], replicated, may hold values from -0.109375 to 0.109375
- picked_unit_indices: int32 [8192, 2], P('seq'), may hold values from 0 to 31, all different within a row; in each aligned block of 256 rows (0 to 255, 256 to 511, ...) at most 24 rows name the same one
- expert_up_weight: bfloat16 [32, 3072, 5120], P('seq', None, 'tp'), may hold values from -0.109375 to 0.109375
- down_weight: bfloat16 [32, 5120, 3072], P('seq', 'tp'), may hold values from -0.125 to 0.125
Outputs:
- mixed: bfloat16 [8192, 3072], P('seq', 'tp')
Inputs may be any that keep to these rules, and one draw needn't show every extreme that they name: `picked_unit_indices`: each row names 2 different experts. Among the rows of one slab of 256 positions no expert is named by more than 24 rows, and in every draw some expert is named by exactly 24 rows of some slab.
All inputs are finite; a program needn't handle non-finite values.
Results may differ from a plain program's by a relative error of at most 0.006.
Values may be sent and summed in bfloat16 or wider, within the bound.
A program may use at most 64 MiB of HBM per device.

v0:
```python
import jax
import jax.numpy as jnp
from jax import lax
from jax.sharding import PartitionSpec as P

EPSILON = 1e-05


def carried_in(shard, axis, combine, identity):
    count, place = (lax.axis_size(axis), lax.axis_index(axis))
    everything = jax.tree.map(lambda part: lax.all_gather(part, axis), shard)
    start = jax.tree.map(
        lambda part, zero: jnp.broadcast_to(jnp.asarray(zero, part.dtype), part.shape),
        shard,
        identity,
    )

    def lap(k, before):
        reached = k < place
        new = combine(before, jax.tree.map(lambda part: part[k], everything))
        return jax.tree.map(lambda a, b: jnp.where(reached, a, b), new, before)

    return lax.fori_loop(0, count, lap, start)


def head_norm(head_values):
    return head_values * lax.rsqrt(
        jnp.mean(head_values * head_values, axis=-1, keepdims=True) + EPSILON
    )


def combine_states(earlier, later):
    return (earlier[0] * later[0], later[0][:, None, None] * earlier[1] + later[1])


def mix_shares(logits, picked_unit_indices):
    gate_values = jax.nn.sigmoid(logits)
    picked_mask = (
        picked_unit_indices[:, :, None]
        == jnp.arange(logits.shape[1], dtype=jnp.int32)[None, None, :]
    )
    chosen = jnp.sum(jnp.where(picked_mask, gate_values[:, None, :], 0.0), axis=2)
    return chosen / jnp.sum(chosen, axis=1, keepdims=True)


def body(
    queries,
    keys,
    values,
    log_decay,
    residual,
    out_weight,
    prenorm_multiplier,
    router_weight,
    picked_unit_indices,
    expert_up_weight,
    down_weight,
):
    slab_rows = queries.shape[0]
    heads_here = log_decay.shape[0]
    head_width = queries.shape[1] // heads_here
    query_heads = queries.reshape(slab_rows, heads_here, head_width)
    key_heads = keys.reshape(slab_rows, heads_here, head_width)
    value_heads = values.reshape(slab_rows, heads_here, head_width)
    cumulative = jnp.cumsum(log_decay, axis=1)
    slab_total = cumulative[:, -1]
    weighted_keys = (
        key_heads.astype(jnp.float32) * jnp.exp(slab_total[None, :] - cumulative.T)[:, :, None]
    )
    updated_memory_matrix = jnp.einsum(
        "thd,the->hde",
        weighted_keys,
        value_heads.astype(jnp.float32),
        precision=lax.Precision.HIGHEST,
    )
    identity = (
        jnp.ones((heads_here,), jnp.float32),
        jnp.zeros((heads_here, head_width, head_width), jnp.float32),
    )
    entering = carried_in(
        (jnp.exp(slab_total), updated_memory_matrix), "seq", combine_states, identity
    )[1]
    position = jnp.arange(slab_rows, dtype=jnp.int32)
    causal = (position[:, None] >= position[None, :])[None]
    log_gap = jnp.where(causal, cumulative[:, :, None] - cumulative[:, None, :], 0.0)
    decay_matrix = jnp.where(causal, jnp.exp(log_gap), 0.0)
    scores = jnp.einsum("thd,shd->hts", query_heads, key_heads, preferred_element_type=jnp.float32)
    intra_weights = (scores * decay_matrix).astype(jnp.bfloat16)
    within_slab = jnp.einsum(
        "hts,she->the", intra_weights, value_heads, preferred_element_type=jnp.float32
    )
    from_state = jnp.einsum(
        "thd,hde->the", query_heads.astype(jnp.float32), entering, precision=lax.Precision.HIGHEST
    )
    head_out = within_slab + from_state * jnp.exp(cumulative).T[:, :, None]
    attention = head_norm(head_out).astype(jnp.bfloat16).reshape(slab_rows, heads_here * head_width)
    projected = jnp.dot(attention, out_weight, preferred_element_type=jnp.float32)
    hidden_state = residual.astype(jnp.float32) + lax.psum_scatter(
        projected, "tp", scatter_dimension=1, tiled=True
    )
    square_sum = lax.psum(jnp.sum(hidden_state * hidden_state, axis=1), "tp")
    inverse_rms = lax.rsqrt(square_sum / out_weight.shape[1] + EPSILON)
    normed = (hidden_state * inverse_rms[:, None] * prenorm_multiplier).astype(jnp.bfloat16)
    expert_count = router_weight.shape[1]
    capacity = 3 * slab_rows // expert_count
    flat_ids = picked_unit_indices.reshape(-1)
    onehot = (flat_ids[:, None] == jnp.arange(expert_count, dtype=jnp.int32)[None, :]).astype(
        jnp.int32
    )
    slot_index = jnp.sum((jnp.cumsum(onehot, axis=0) - onehot) * onehot, axis=1)
    target = flat_ids * capacity + slot_index
    choices_per_row = picked_unit_indices.shape[1]
    full_rows = lax.all_gather(normed, "tp", axis=1, tiled=True)
    shares = mix_shares(
        jnp.dot(full_rows, router_weight, preferred_element_type=jnp.float32), picked_unit_indices
    )
    outgoing = jnp.zeros((expert_count * capacity, full_rows.shape[1]), jnp.bfloat16)
    outgoing = outgoing.at[target].set(jnp.repeat(full_rows, choices_per_row, axis=0))
    outgoing = outgoing.reshape(expert_count, capacity, full_rows.shape[1])
    arrived = lax.all_to_all(outgoing, "seq", split_axis=0, concat_axis=0, tiled=True)
    row_block = arrived.reshape(-1, arrived.shape[2])
    hidden = jax.nn.silu(
        jnp.dot(row_block, expert_up_weight[0], preferred_element_type=jnp.float32)
    ).astype(jnp.bfloat16)
    partial_value = jnp.dot(hidden, down_weight[0], preferred_element_type=jnp.float32).astype(
        jnp.bfloat16
    )
    returned = lax.all_to_all(
        partial_value.reshape(arrived.shape), "seq", split_axis=0, concat_axis=0, tiled=True
    )
    picked = returned.reshape(expert_count * capacity, -1)[target].reshape(
        slab_rows, choices_per_row, -1
    )
    weighted = jnp.sum(shares[:, :, None] * picked, axis=1)
    expert_mix = lax.psum_scatter(weighted, "tp", scatter_dimension=1, tiled=True)
    return (hidden_state + expert_mix).astype(jnp.bfloat16)


def solution(mesh):
    in_specs = (
        P("seq", "tp"),
        P("seq", "tp"),
        P("seq", "tp"),
        P("tp", "seq"),
        P("seq", "tp"),
        P("tp", None),
        P("tp"),
        P(),
        P("seq", None),
        P("seq", None, "tp"),
        P("seq", "tp", None),
    )
    out_specs = P("seq", "tp")
    return jax.shard_map(body, mesh=mesh, in_specs=in_specs, out_specs=out_specs, check_vma=False)
```

profile of v0, /device:TPU:2, one launch (start us, length us, event | category | flops | bytes accessed | tf_op | source)
XLA Modules:
  0.0 553.6 jit_solution(14559209757030952898)
XLA Ops:
  6.5 0.8 reshape.169
  7.4 1.2 reduce-window.14
  9.2 1.1 copy.69
  10.3 2.2 fusion.18
  12.6 1.2 dynamic-slice
  14.6 74.2 %all-reduce = f32[128]{0:T(128)S(1)} all-reduce(f32[128]{0:T(128)S(1)} %bitcast_dynamic-update-slice_fusion), channel_id=2, replica_groups=mesh['seq'=32,'tp'=8] {'seq'}, use_global_device_ids=true, to_apply=%add | all-reduce | flops 128 | bytes 1024
  88.9 2.6 convolution_bitcast_fusion.1
  91.5 21.6 %all-gather.7.cloned.1.call-done = f32[128,128,128]{2,1,0:T(8,128)} async-done(((f32[4,128,128]{2,1,0:T(8,128)}), f32[128,128,128]{2,1,0:T(8,128)}) %all-gather.7.cloned.1.call-update) | async-done | bytes 8388624 | tf_op jit(solution)/shard_map/all_gather | solution.py:11
  113.0 35.1 %while.14 = (s32[]{:T(128)}, f32[4,128,128]{2,1,0:T(8,128)S(1)}, s32[]{:T(128)}, f32[32,4]{1,0:T(8,128)S(1)}, f32[32,4,128,128]{3,2,1,0:T(8,128)}, /*index=5*/s32[]{:T(128)}, s32[]{:T(128)}) while((s32[]{:T(128)}, f32[4,128,128]{2,1,0:T(8,128)S(1)}, s32[]{:T(128)}, f32[32,4]{1,0:T(8,128)S(1)}, f32[32,4,128,128]{3,2,1,0:T(8,128)}, ...), condition=%wide.region_3.4_spmd.clone, body=%wide.region_2.3_spmd.clone.sunk | while | flops 262148 | bytes 786593 | solution.py:23
  113.0 1.0 fusion.55
  114.1 1.1 fusion.55
  115.2 1.1 fusion.55
  116.3 1.1 fusion.55
  117.4 1.1 fusion.55
  118.5 1.1 fusion.55
  119.6 1.1 fusion.55
  120.7 1.1 fusion.55
  121.8 1.1 fusion.55
  122.9 1.1 fusion.55
  124.0 1.1 fusion.55
  125.1 1.1 fusion.55
  126.2 1.1 fusion.55
  127.3 1.1 fusion.55
  128.4 1.1 fusion.55
  129.5 1.1 fusion.55
  130.6 1.1 fusion.55
  131.7 1.1 fusion.55
  132.8 1.1 fusion.55
  133.9 1.1 fusion.55
  135.0 1.1 fusion.55
  136.1 1.1 fusion.55
  137.2 1.1 fusion.55
  138.3 1.1 fusion.55
  139.4 1.1 fusion.55
  140.5 1.1 fusion.55
  141.6 1.1 fusion.55
  142.7 1.1 fusion.55
  143.8 1.1 fusion.55
  144.9 1.1 fusion.55
  146.0 1.1 fusion.55
  147.1 1.1 fusion.55
  148.1 1.6 multiply_reduce_fusion.1
  149.8 2.7 fusion.41
  152.6 36.7 %reduce-scatter.3.cloned.1.call-done = f32[256,384]{1,0:T(8,128)} async-done(((f32[256,3072]{1,0:T(8,128)}), f32[256,384]{1,0:T(8,128)}) %reduce-scatter.3.cloned.1.call-update) | async-done | bytes 393232 | tf_op jit(solution)/shard_map/reduce_scatter | solution.py:98
  189.2 1.1 multiply_reduce_fusion.2
  190.4 12.9 %psum.7 = f32[256]{0:T(256)S(1)} all-reduce(f32[256]{0:T(256)S(1)} %multiply_reduce_fusion.2), channel_id=1, replica_groups=mesh['seq'=32,'tp'=8] {'tp'}, use_global_device_ids=true, to_apply=%region_7.8 | all-reduce | flops 256 | bytes 2048 | tf_op jit(solution)/shard_map/psum | solution.py:101
  203.3 1.8 multiply_convert_fusion.2
  205.8 1.2 reduce-window.16
  207.4 23.8 %all-gather.5.cloned.1.call-done = bf16[256,3072]{1,0:T(8,128)(2,1)} async-done(((bf16[256,384]{1,0:T(8,128)(2,1)}), bf16[256,3072]{1,0:T(8,128)(2,1)}) %all-gather.5.cloned.1.call-update) | async-done | bytes 1572880 | tf_op jit(solution)/shard_map/all_gather | solution.py:113
  231.2 3.0 broadcast_in_dim.63
  234.3 2.7 reshape.192
  237.0 9.0 %scatter_custom_fusion = bf16[768,3072]{1,0:T(8,128)(2,1)} fusion(s32[512]{0:T(512)S(1)} %bitcast.118, bf16[512,3072]{1,0:T(8,128)(2,1)} %reshape.192, bf16[]{:T(256)} %constant.57.clone.1), kind=kCustom, calls=%fused_computation.10 | custom fusion | bytes 4719104 | tf_op jit(solution)/shard_map/scatter | solution.py:118
  246.0 117.5 %all_to_all.10 = bf16[32,24,3072]{2,1,0:T(8,128)(2,1)S(1)} all-to-all(bf16[32,24,3072]{2,1,0:T(8,128)(2,1)} %bitcast.109), channel_id=1, replica_groups=mesh['seq'=32,'tp'=8] {'seq'}, dimensions={0} | all-to-all | bytes 9437184 | tf_op jit(solution)/shard_map/all_to_all | solution.py:120
  363.5 4.0 multiply_convert_fusion
  367.5 5.6 %convolution_convert_fusion = bf16[768,3072]{1,0:T(8,128)(2,1)} fusion(bf16[768,640]{1,0:T(8,128)(2,1)S(1)} %multiply_convert_fusion, bf16[1,640,3072]{2,1,0:T(8,128)(2,1)S(1)} %copy-done.10), kind=kOutput, calls=%fused_computation.6 | convolution fusion | flops 3022258176 | bytes 9633792 | tf_op jit(solution)/shard_map/dot_general | solution.py:125
  373.2 5.7 %all-to-all-start.1 = ((bf16[32,24,3072]{2,1,0:T(8,128)(2,1)}), bf16[32,24,3072]{2,1,0:T(8,128)(2,1)}, u32[]{:S(2)}, u32[]{:S(2)}) async-start(bf16[32,24,3072]{2,1,0:T(8,128)(2,1)} %bitcast.110), calls=%async_computation.2 | async-start | bytes 9437184 | tf_op jit(solution)/shard_map/all_to_all | solution.py:128
  379.2 0.6 fusion.13
  379.8 0.8 copy.62
  380.7 102.1 %all-to-all-done.1 = bf16[32,24,3072]{2,1,0:T(8,128)(2,1)} async-done(((bf16[32,24,3072]{2,1,0:T(8,128)(2,1)}), bf16[32,24,3072]{2,1,0:T(8,128)(2,1)}, u32[]{:S(2)}, u32[]{:S(2)}) %all-to-all-start.1) | async-done | bytes 4718624 | tf_op jit(solution)/shard_map/all_to_all | solution.py:128
  482.8 9.0 %gather_fusion = bf16[512,3072]{1,0:T(8,128)(2,1)S(1)} fusion(bf16[768,3072]{1,0:T(8,128)(2,1)} %bitcast.18, s32[1024]{0:T(1024)S(1)} %pad_clamp_fusion), kind=kCustom, calls=%fused_computation | custom fusion | bytes 6293504 | tf_op jit(solution)/shard_map/gather | solution.py:131
  491.8 5.3 reshape.179
  497.1 12.1 %multiply_reduce_fusion = f32[256,3072]{1,0:T(8,128)} fusion(f32[256,2,3072]{2,1,0:T(2,128)} %reshape.179, f32[256,2]{1,0:T(8,128)} %copy.62), kind=kLoop, calls=%fused_computation.5 | loop fusion | flops 2359296 | bytes 9439232 | tf_op jit(solution)/shard_map/reduce_sum | solution.py:134
  509.2 36.1 %reduce-scatter.5.cloned.1.call-done = f32[256,384]{1,0:T(8,128)} async-done(((f32[256,3072]{1,0:T(8,128)}), f32[256,384]{1,0:T(8,128)}) %reduce-scatter.5.cloned.1.call-update) | async-done | bytes 393232 | tf_op jit(solution)/shard_map/reduce_scatter | solution.py:135
  545.3 1.8 add_convert_fusion
  (95 shorter events, 2.8 us)
Async XLA Ops:
  6.5 143.3 %copy-start = (bf16[512,3072]{1,0:T(8,128)(2,1)S(1)}, bf16[512,3072]{1,0:T(8,128)(2,1)}, u32[]{:S(2)}) copy-start(bf16[512,3072]{1,0:T(8,128)(2,1)} %param.18) | copy-start | bytes 9437188
  6.5 106.5 %all-gather.7.cloned.1.call-start = ((), (), s32[]{:S(2)}) async-start(), calls=%async_computation.7 | async-start | bytes 8650752 | tf_op jit(solution)/shard_map/all_gather | solution.py:11
  10.3 2.3 copy-start.5
  12.5 176.7 %reduce-scatter.3.cloned.1.call-start = ((), (), s32[]{:S(2)}) async-start(), calls=%async_computation.4 | async-start | bytes 3538944 | tf_op jit(solution)/shard_map/reduce_scatter | solution.py:98
  149.8 39.4 %copy-start.4 = (bf16[256,384]{1,0:T(8,128)(2,1)S(1)}, bf16[256,384]{1,0:T(8,128)(2,1)}, u32[]{:S(2)}) copy-start(bf16[256,384]{1,0:T(8,128)(2,1)} %param.17) | copy-start | bytes 589828
  149.8 53.5 %copy-start.8 = (f32[384]{0:T(512)S(1)}, f32[384]{0:T(512)}, u32[]{:S(2)}) copy-start(f32[384]{0:T(512)} %param.19) | copy-start | bytes 4612
  152.5 52.6 %copy-start.7 = (s32[256,2]{0,1:T(2,128)S(1)}, s32[256,2]{0,1:T(2,128)}, u32[]{:S(2)}) copy-start(s32[256,2]{0,1:T(2,128)} %param.21) | copy-start | bytes 6148
  152.5 78.7 %all-gather.5.cloned.1.call-start = ((), (), s32[]{:S(2)}) async-start(), calls=%async_computation.5 | async-start | bytes 1769472 | tf_op jit(solution)/shard_map/all_gather | solution.py:113
  246.0 117.5 %copy-start.9 = (bf16[1,3072,640]{2,1,0:T(8,128)(2,1)S(1)}, bf16[1,3072,640]{2,1,0:T(8,128)(2,1)}, u32[]{:S(2)}) copy-start(bf16[1,3072,640]{2,1,0:T(8,128)(2,1)} %param.22) | copy-start | bytes 11796484
  363.5 4.0 copy-start.10
  373.1 6.0 %copy-start.2 = (bf16[256,3072]{1,0:T(8,128)(2,1)S(1)}, bf16[256,3072]{1,0:T(8,128)(2,1)}, u32[]{:S(2)}) copy-start(bf16[256,3072]{1,0:T(8,128)(2,1)} %all-gather.5.cloned.1.call-done) | copy-start | bytes 4718596
  373.2 6.0 %copy-start.6 = (bf16[3072,32]{0,1:T(8,128)(2,1)S(1)}, bf16[3072,32]{0,1:T(8,128)(2,1)}, u32[]{:S(2)}) copy-start(bf16[3072,32]{0,1:T(8,128)(2,1)} %param.20) | copy-start | bytes 589828
  373.2 109.6 %all-to-all-start.1 = ((bf16[32,24,3072]{2,1,0:T(8,128)(2,1)}), bf16[32,24,3072]{2,1,0:T(8,128)(2,1)}, u32[]{:S(2)}, u32[]{:S(2)}) async-start(bf16[32,24,3072]{2,1,0:T(8,128)(2,1)} %bitcast.110), calls=%async_computation.2 | async-start | bytes 9437184 | tf_op jit(solution)/shard_map/all_to_all | solution.py:128
  378.9 166.4 %reduce-scatter.5.cloned.1.call-start = ((), (), s32[]{:S(2)}) async-start(), calls=%async_computation.6 | async-start | bytes 3538944 | tf_op jit(solution)/shard_map/reduce_scatter | solution.py:135
  497.1 48.2 %copy-start.3 = (f32[256,384]{1,0:T(8,128)S(1)}, f32[256,384]{1,0:T(8,128)}, u32[]{:S(2)}) copy-start(f32[256,384]{1,0:T(8,128)} %reduce-scatter.3.cloned.1.call-done) | copy-start | bytes 1179652
  497.1 50.0 %copy-start.1 = (bf16[512,3072]{1,0:T(8,128)(2,1)S(1)}, bf16[512,3072]{1,0:T(8,128)(2,1)}, u32[]{:S(2)}) copy-start(bf16[512,3072]{1,0:T(8,128)(2,1)} %param.18) | copy-start | bytes 9437188
Sparse Core Ops, SparseCore 0:
  12.7 100.3 all-gather.6
  152.6 36.5 reduce-scatter.2
  205.2 25.9 all-gather.4
  509.3 35.9 reduce-scatter.4
where the time goes:
time: 555 us; the launch traced here: 554 us
  waiting for transfers between devices  220 us (40%)
  blocking collectives  205 us (37%)
  other arithmetic  53.4 us (10%)
  local copies, waits for them, and re-layouts  35 us (6%)
  matrix products  19.2 us (3%)
  between operations  14 us (3%)
  starting transfers between devices  6.09 us (1%)
    all_to_all x1, blocking collectives, body(): lax.all_to_all(outgoing, 'seq', split_axis=0, concat_axis=0, tiled=True)  118 us
    all_to_all x1, waiting for transfers between devices, body(): lax.all_to_all(partial_value.reshape(arrived.shape), 'seq', split_axis=0,...  102 us
    unnamed x1, blocking collectives  74.2 us
    reduce_scatter x1, waiting for transfers between devices, body(): lax.psum_scatter(projected, 'tp', scatter_dimension=1, tiled=True)  36.7 us
    reduce_scatter x1, waiting for transfers between devices, body(): lax.psum_scatter(weighted, 'tp', scatter_dimension=1, tiled=True)  36.1 us
    select_n x32, other arithmetic, lap(): return jax.tree.map(lambda a, b: jnp.where(reached, a, b), new, before)  33.8 us
    all_gather x1, waiting for transfers between devices, body(): full_rows = lax.all_gather(normed, 'tp', axis=1, tiled=True)  23.8 us
    all_gather x1, waiting for transfers between devices, carried_in(): everything = jax.tree.map(lambda part: lax.all_gather(part, axis), shard)  21.6 us
  transfers between devices with their start and end apart: 5, of which 5 were waited for; matrix products, arithmetic and copies ran while one was open for 1% of the time, Pallas kernels for 0%

commit v1 on v0

v1 whole, which is shorter than its diff:
```python
import functools

import jax
import jax.numpy as jnp
from jax import lax
from jax.experimental import pallas as pl
from jax.experimental.pallas import tpu as pltpu
from jax.sharding import PartitionSpec as P

EPSILON = 1e-05
MESH = pl.DeviceIdType.MESH
F32, BF16 = jnp.float32, jnp.bfloat16
HIGHEST = lax.Precision.HIGHEST
CAP = 24
PAD = 32
CORES = 2


def mm(a, b):
    return jnp.dot(a, b, preferred_element_type=F32)


def mm_nt(a, b):
    return lax.dot_general(a, b, (((1,), (1,)), ((), ())), preferred_element_type=F32)


def mm_tn(a, b):
    return lax.dot_general(a, b, (((0,), (0,)), ((), ())), preferred_element_type=F32)


def iota(shape, dim):
    return lax.broadcasted_iota(jnp.int32, shape, dim)


def flag(mask):
    return jnp.where(mask, 1.0, 0.0).astype(BF16)


def split2(x):
    high = x.astype(BF16)
    return high, (x - high.astype(F32)).astype(BF16)


def to_column(row):
    n = row.shape[1]
    eye = iota((n, n), 0) == iota((n, n), 1)
    return jnp.sum(jnp.where(eye, row, 0.0), axis=1, keepdims=True)


def to_row(column):
    n = column.shape[0]
    eye = iota((n, n), 0) == iota((n, n), 1)
    return jnp.sum(jnp.where(eye, column, 0.0), axis=0, keepdims=True)


def send(src, dst, send_sem, recv_sem, device):
    pltpu.make_async_remote_copy(
        src_ref=src,
        dst_ref=dst,
        send_sem=send_sem,
        recv_sem=recv_sem,
        device_id=device,
        device_id_type=MESH,
    ).start()


def wait(ref, sem):
    pltpu.make_async_copy(ref, ref, sem).wait()


def scratch_of(c):
    n, y, g, w, t, hd = c["n"], c["y"], c["g"], c["w"], c["t"], c["hd"]
    tp, slots, rows, padded, f = y * CORES, c["slots"], c["rows"], c["padded"], c["f"]
    dma = pltpu.SemaphoreType.DMA
    return dict(
        owv=pltpu.VMEM((tp, c["a"], w), BF16),
        rwv=pltpu.VMEM((w, n), BF16),
        upv=pltpu.VMEM((y, CORES * w, f), BF16),
        dnv=pltpu.VMEM((y, f, CORES * w), BF16),
        ub=pltpu.VMEM((n, hd, 128), BF16),
        ur=pltpu.VMEM((n, hd, 128), BF16),
        ts=pltpu.VMEM((c["heads"], 1, 128), F32),
        tr=pltpu.VMEM((n, 1, 128), F32),
        sb=pltpu.VMEM((n, hd, 128), BF16),
        se=pltpu.VMEM((n, hd, 128), BF16),
        within=pltpu.VMEM((t, c["a"]), F32),
        ps1=pltpu.VMEM((y, t, w), BF16),
        pr1=pltpu.VMEM((y, t, w), BF16),
        ps2=pltpu.VMEM((y, t, w), BF16),
        pr2=pltpu.VMEM((y, t, w), BF16),
        sqs=pltpu.VMEM((1, t), F32),
        sqr=pltpu.VMEM((tp, 1, t), F32),
        cs=pltpu.VMEM((2, 1, t), F32),
        cr=pltpu.VMEM((tp, 2, 1, t), F32),
        pm=pltpu.VMEM((n * PAD, t), BF16),
        q0=pltpu.VMEM((t, n * PAD), BF16),
        q1=pltpu.VMEM((t, n * PAD), BF16),
        dsp=pltpu.VMEM((n * PAD, w), BF16),
        xr=pltpu.VMEM((g, padded, w), BF16),
        xg=pltpu.VMEM((g, y, rows, CORES * w), BF16),
        mb=pltpu.VMEM((g, y, rows, w), F32),
        ps=pltpu.VMEM((g, y, rows, w), BF16),
        pr=pltpu.VMEM((g, y, rows, w), BF16),
        ys=pltpu.VMEM((g, y, rows, w), BF16),
        yr=pltpu.VMEM((g, y, rows, w), BF16),
        hs=pltpu.VMEM((g, padded, w), BF16),
        ret=pltpu.VMEM((n * PAD, w), BF16),
        w_ow=dma((tp,)),
        w_up=dma((y,)),
        w_dn=dma((y,)),
        w_rw=dma((1,)),
        m_s=dma((8,)),
        m_r=dma((8,)),
        p1_s=dma((y,)),
        p1_r=dma((y,)),
        p2_s=dma((y,)),
        p2_r=dma((y,)),
        x_s=dma((g,)),
        x_r=dma((g,)),
        a_s=dma((g, y)),
        a_r=dma((g, y)),
        b_s=dma((g, y)),
        b_r=dma((g, y)),
        c_s=dma((g, y)),
        c_r=dma((g, y)),
        d_s=dma((g, y)),
        d_r=dma((g, y)),
        h_s=dma((g,)),
    )


def kernel(c, names, *refs):
    (q, k, v, ld, res, mult, ids, idst, ow, rw, up, dn, out) = refs[:13]
    r = dict(zip(names, refs[13:]))
    n, xs, zs, ys_n, groups = c["n"], c["x"], c["z"], c["y"], c["groups"]
    heads, t, w, hd, tp_n = c["heads"], c["t"], c["w"], c["hd"], c["y"] * CORES
    rows, padded, slots = c["rows"], c["padded"], c["slots"]
    s, tp = lax.axis_index("seq"), lax.axis_index("tp")
    z, x = s // xs, lax.rem(s, xs)
    y, core = tp // CORES, lax.rem(tp, CORES)
    partner = (s, y * CORES + 1 - core)
    m_s, m_r = r["m_s"], r["m_r"]

    def seq_peers(body):
        def step(i, carry):
            body(lax.rem(s + i, n))
            return carry

        lax.fori_loop(1, n, step, 0)

    def tp_peers(body):
        def step(i, carry):
            body(lax.rem(tp + i, tp_n))
            return carry

        lax.fori_loop(1, tp_n, step, 0)

    barrier = pltpu.get_barrier_semaphore()
    seq_peers(
        lambda p: pl.semaphore_signal(barrier, inc=1, device_id=(p, tp), device_id_type=MESH)
    )
    tp_peers(lambda p: pl.semaphore_signal(barrier, inc=1, device_id=(s, p), device_id_type=MESH))

    weights = []
    for u in range(tp_n):
        weights.append(
            pltpu.make_async_copy(ow.at[:, pl.ds(u * w, w)], r["owv"].at[u], r["w_ow"].at[u])
        )
    weights.append(
        pltpu.make_async_copy(
            rw.at[pl.ds(pl.multiple_of(tp * w, w), w), :], r["rwv"], r["w_rw"].at[0]
        )
    )
    for i in range(ys_n):
        part = pl.ds(i * CORES * w, CORES * w)
        weights.append(
            pltpu.make_async_copy(up.at[0, part, :], r["upv"].at[i], r["w_up"].at[i])
        )
    for i in range(ys_n):
        part = pl.ds(i * CORES * w, CORES * w)
        weights.append(
            pltpu.make_async_copy(dn.at[0, :, part], r["dnv"].at[i], r["w_dn"].at[i])
        )
    for copy in weights:
        copy.start()

    logs = ld[...]
    upper = jnp.where(iota((t, t), 0) <= iota((t, t), 1), 1.0, 0.0)
    lower = jnp.where(iota((t, t), 0) >= iota((t, t), 1), 1.0, 0.0)
    c_row = jnp.dot(logs, upper, precision=HIGHEST, preferred_element_type=F32)
    c_col = lax.dot_general(
        lower, logs, (((1,), (1,)), ((), ())), precision=HIGHEST, preferred_element_type=F32
    )
    per_head = 128 // hd
    for h in range(heads):
        head = pl.ds(h * 128, 128)
        total = c_row[h : h + 1, t - 1 : t]
        r["ts"][h] = jnp.broadcast_to(total, (1, 128))
        weighted = k[:, head].astype(F32) * jnp.exp(total - c_col[:, h : h + 1])
        high, low = split2(weighted)
        product = (mm_tn(high, v[:, head]) + mm_tn(low, v[:, head])).astype(BF16)
        for i in range(per_head):
            r["ub"][h * per_head + i] = product[i * hd : (i + 1) * hd]

    pl.semaphore_wait(barrier, n - 1 + tp_n - 1)

    ub, ur, ts, tr, sb, se = (r[name] for name in ("ub", "ur", "ts", "tr", "sb", "se"))
    seq_peers(lambda p: send(ts.at[p // per_head], tr.at[s], m_s.at[0], m_r.at[0], (p, tp)))
    seq_peers(lambda p: send(ub.at[p], ur.at[s], m_s.at[1], m_r.at[1], (p, tp)))
    tr[s] = ts[s // per_head]
    ur[s] = ub[s]

    ids_c = ids[...]
    ids_r = idst[...]
    first, second = ids_c[:, 0:1], ids_c[:, 1:2]
    names_lane = iota((t, n), 1)
    before = flag(iota((t, t), 1) < iota((t, t), 0))
    counts = mm(before, flag((first == names_lane) | (second == names_lane)))
    for j, pick, q_ref in ((0, first, r["q0"]), (1, second, r["q1"])):
        slot = jnp.sum(jnp.where(pick == names_lane, counts, 0.0), axis=1, keepdims=True)
        target = pick.astype(F32) * PAD + slot
        q_ref[...] = flag(iota((t, n * PAD), 1).astype(F32) == target)
    first, second = ids_r[0:1, :], ids_r[1:2, :]
    names_sub = iota((n, t), 0)
    after = flag(iota((t, t), 0) < iota((t, t), 1))
    counts = mm(flag((first == names_sub) | (second == names_sub)), after)
    targets = []
    for pick in (first, second):
        slot = jnp.sum(jnp.where(pick == names_sub, counts, 0.0), axis=0, keepdims=True)
        targets.append(pick.astype(F32) * PAD + slot)
    place = iota((n * PAD, t), 0).astype(F32)
    r["pm"][...] = flag((place == targets[0]) | (place == targets[1]))

    causal = iota((t, t), 0) >= iota((t, t), 1)
    for h in range(heads):
        head = pl.ds(h * 128, 128)
        scores = mm_nt(q[:, head], k[:, head])
        gap = jnp.where(causal, c_col[:, h : h + 1] - c_row[h : h + 1, :], 0.0)
        intra = jnp.where(causal, scores * jnp.exp(gap), 0.0).astype(BF16)
        r["within"][:, head] = mm(intra, v[:, head])

    wait(tr.at[pl.ds(0, n - 1)], m_r.at[0])
    wait(ur.at[pl.ds(0, n - 1)], m_r.at[1])

    def scan(b, state):
        sb[b] = state.astype(BF16)
        return jnp.exp(tr[b]) * state + ur[b].astype(F32)

    lax.fori_loop(0, n, scan, jnp.zeros((hd, 128), F32))
    seq_peers(lambda p: send(sb.at[p], se.at[s], m_s.at[2], m_r.at[2], (p, tp)))
    se[s] = sb[s]
    wait(se.at[pl.ds(0, n - 1)], m_r.at[2])

    attended = []
    for h in range(heads):
        head = pl.ds(h * 128, 128)
        state = se[h * per_head : (h + 1) * per_head].reshape(128, 128)
        head_out = r["within"][:, head] + mm(q[:, head], state) * jnp.exp(c_col[:, h : h + 1])
        mean = jnp.mean(head_out * head_out, axis=1, keepdims=True)
        attended.append((head_out * lax.rsqrt(mean + EPSILON)).astype(BF16))
    attention = jnp.concatenate(attended, axis=1)

    ps1, pr1, ps2, pr2 = (r[name] for name in ("ps1", "pr1", "ps2", "pr2"))
    for copy in weights[: tp_n + 1]:
        copy.wait()
    order = [d for d in (2, 1, 3) if d < ys_n] + [0]
    for d in order:
        to = lax.rem(y + d, ys_n)
        ps1[to] = mm(attention, r["owv"][to * CORES + 1 - core]).astype(BF16)
        send(ps1.at[to], pr1.at[to], r["p1_s"].at[to], r["p1_r"].at[to], partner)
    hidden = res[...].astype(F32)
    for d in order:
        to = lax.rem(y + d, ys_n)
        mine = mm(attention, r["owv"][to * CORES + core])
        wait(pr1.at[to], r["p1_r"].at[to])
        mine = mine + pr1[to].astype(F32)
        if d:
            ps2[d] = mine.astype(BF16)
            send(ps2.at[d], pr2.at[d], r["p2_s"].at[d], r["p2_r"].at[d], (s, to * CORES + core))
        else:
            hidden = hidden + mine
    for d in order[:-1]:
        wait(pr2.at[d], r["p2_r"].at[d])
        hidden = hidden + pr2[d].astype(F32)

    sqs, sqr = r["sqs"], r["sqr"]
    high, low = split2(hidden * hidden)
    ones = jnp.ones((8, w), BF16)
    sqs[...] = (mm_nt(ones, high) + mm_nt(ones, low))[0:1]
    tp_peers(lambda p: send(sqs, sqr.at[tp], m_s.at[3], m_r.at[3], (s, p)))
    sqr[tp] = sqs[...]
    wait(sqr.at[pl.ds(0, tp_n - 1)], m_r.at[3])
    square_sum = sqr[0]
    for u in range(1, tp_n):
        square_sum = square_sum + sqr[u]
    inverse = to_column(lax.rsqrt(square_sum / (w * tp_n) + EPSILON))
    normed = (hidden * inverse * mult[...]).astype(BF16)

    dsp, xr, ret = r["dsp"], r["xr"], r["ret"]
    dsp[...] = mm(r["pm"][...], normed).astype(BF16)

    def rows_of(index):
        return pl.ds(pl.multiple_of(index * PAD, PAD), PAD)

    def group_peers(g, sign, body):
        near, far = groups[g]

        def step(j, carry):
            dz = jnp.where(j < xs, near, far)
            dx = lax.rem(j, xs)
            pz = lax.rem(z + zs + sign * dz, zs)
            px = lax.rem(x + xs + sign * dx, xs)
            body(j, pz * xs + px)
            return carry

        lax.fori_loop(0 if near else 1, slots, step, 0)

    for g in range(len(groups)):
        group_peers(
            g,
            1,
            lambda j, p, g=g: send(
                dsp.at[rows_of(p)], xr.at[g, rows_of(j)], r["x_s"].at[g], r["x_r"].at[g], (p, tp)
            ),
        )
    last = len(groups) - 1
    xr[last, 0:PAD] = dsp[rows_of(s)]

    cs, cr = r["cs"], r["cr"]
    logits = mm(normed, r["rwv"][...])
    for j in range(2):
        chosen = jnp.where(ids_c[:, j : j + 1] == names_lane, logits, 0.0)
        cs[j] = to_row(jnp.sum(chosen, axis=1, keepdims=True))
    tp_peers(lambda p: send(cs, cr.at[tp], m_s.at[4], m_r.at[4], (s, p)))
    cr[tp] = cs[...]

    xg, mb, ps, pr, ys, yr, hs = (r[name] for name in ("xg", "mb", "ps", "pr", "ys", "yr", "hs"))
    compact_row, compact_lane = iota((rows, padded), 0), iota((rows, padded), 1)
    block = (compact_row * 2731) >> 16
    pack = flag(compact_lane == block * PAD + (compact_row - block * CAP))
    spread_row, spread_lane = iota((padded, rows), 0), iota((padded, rows), 1)
    block = (spread_lane * 2731) >> 16
    spread = flag(spread_row == block * PAD + (spread_lane - block * CAP))
    own_half = pl.ds(pl.multiple_of(core * w, w), w)
    other_half = pl.ds(pl.multiple_of((1 - core) * w, w), w)
    arrive = [d for d in (1, 3, 2) if d < ys_n]

    def spread_out(g):
        ref = xr.at[g] if groups[g][0] else xr.at[g, pl.ds(0, padded - PAD)]
        wait(ref, r["x_r"].at[g])
        packed = mm(pack, xr[g]).astype(BF16)
        for side in range(CORES):

            @pl.when(core == side)
            def _(side=side):
                xg[g, y, :, side * w : (side + 1) * w] = packed

        piece = xg.at[g, y, :, own_half]
        for d in order[:-1]:
            to = lax.rem(y + d, ys_n)
            send(piece, piece, r["a_s"].at[g, d], r["a_r"].at[g, d], (s, to * CORES + core))
        send(piece, piece, r["b_s"].at[g, 0], r["b_r"].at[g, 0], partner)

    def hand_over(g):
        for d in arrive:
            piece = xg.at[g, lax.rem(y + ys_n - d, ys_n), :, own_half]
            wait(piece, r["a_r"].at[g, d])
            send(piece, piece, r["b_s"].at[g, d], r["b_r"].at[g, d], partner)

    def expert(g):
        for d in range(ys_n):
            wait(
                xg.at[g, lax.rem(y + ys_n - d, ys_n), :, other_half],
                r["b_r"].at[g, d],
            )
        total = mm(xg[g, 0], r["upv"][0])
        for i in range(1, ys_n):
            total = total + mm(xg[g, i], r["upv"][i])
        hidden_rows = (total / (1.0 + jnp.exp(-total))).astype(BF16)
        for i in range(ys_n):
            part = mm(hidden_rows, r["dnv"][i])
            left, right = part[:, :w], part[:, w:]
            mb[g, i] = jnp.where(core == 0, left, right)
            ps[g, i] = jnp.where(core == 0, right, left).astype(BF16)
            send(ps.at[g, i], pr.at[g, i], r["c_s"].at[g, i], r["c_r"].at[g, i], partner)

    def over_y(g):
        for d in order[:-1]:
            to = lax.rem(y + d, ys_n)
            wait(pr.at[g, to], r["c_r"].at[g, to])
            ys[g, d] = (mb[g, to] + pr[g, to].astype(F32)).astype(BF16)
            send(
                ys.at[g, d],
                yr.at[g, d],
                r["d_s"].at[g, d],
                r["d_r"].at[g, d],
                (s, to * CORES + core),
            )

    def home(g):
        wait(pr.at[g, y], r["c_r"].at[g, y])
        total = mb[g, y] + pr[g, y].astype(F32)
        for d in arrive:
            wait(yr.at[g, d], r["d_r"].at[g, d])
            total = total + yr[g, d].astype(F32)
        hs[g] = mm(spread, total.astype(BF16)).astype(BF16)
        group_peers(
            g,
            -1,
            lambda j, p: send(
                hs.at[g, rows_of(j)], ret.at[rows_of(s)], r["h_s"].at[g], m_r.at[5], (p, tp)
            ),
        )
        if not groups[g][0]:
            ret[rows_of(s)] = hs[g, 0:PAD]

    for copy in weights[tp_n + 1 :]:
        copy.wait()
    stages = (spread_out, hand_over, expert, over_y, home)
    for step in range(len(groups) + len(stages) - 1):
        for lag, stage in enumerate(stages):
            if 0 <= step - lag < len(groups):
                stage(step - lag)

    wait(cr.at[pl.ds(0, tp_n - 1)], m_r.at[4])
    gates = []
    for j in range(2):
        logit = cr[0, j]
        for u in range(1, tp_n):
            logit = logit + cr[u, j]
        gates.append(jax.nn.sigmoid(logit))
    both = gates[0] + gates[1]
    shares = [to_column(gate / both) for gate in gates]
    wait(ret.at[pl.ds(0, (n - 1) * PAD)], m_r.at[5])
    returned = ret[...]
    mix = shares[0] * mm(r["q0"][...], returned) + shares[1] * mm(r["q1"][...], returned)
    out[...] = (hidden + mix).astype(BF16)

    wait(tr.at[pl.ds(0, n - 1)], m_s.at[0])
    wait(ur.at[pl.ds(0, n - 1)], m_s.at[1])
    wait(se.at[pl.ds(0, n - 1)], m_s.at[2])
    wait(sqr.at[pl.ds(0, tp_n - 1)], m_s.at[3])
    wait(cr.at[pl.ds(0, tp_n - 1)], m_s.at[4])
    for i in range(ys_n):
        wait(ps1.at[i], r["p1_s"].at[i])
    for d in order[:-1]:
        wait(ps2.at[d], r["p2_s"].at[d])
    for g in range(len(groups)):
        ref = xr.at[g] if groups[g][0] else xr.at[g, pl.ds(0, padded - PAD)]
        wait(ref, r["x_s"].at[g])
        wait(ref, r["h_s"].at[g])
        for d in range(ys_n):
            wait(ps.at[g, d], r["b_s"].at[g, d])
            wait(ps.at[g, d], r["c_s"].at[g, d])
            if d:
                wait(ps.at[g, d], r["a_s"].at[g, d])
                wait(ps.at[g, d], r["d_s"].at[g, d])


def body(
    sizes,
    queries,
    keys,
    values,
    log_decay,
    residual,
    out_weight,
    prenorm_multiplier,
    router_weight,
    picked_unit_indices,
    expert_up_weight,
    down_weight,
):
    n, xs, zs, ys = sizes
    half = zs // 2
    groups = [(d, zs - d) for d in range(1, half)] + [(0, half)]
    heads = log_decay.shape[0]
    slots = 2 * xs
    c = dict(
        n=n,
        x=xs,
        z=zs,
        y=ys,
        groups=groups,
        g=len(groups),
        heads=heads,
        t=queries.shape[0],
        a=queries.shape[1],
        w=residual.shape[1],
        f=expert_up_weight.shape[2],
        hd=heads * 128 // n,
        slots=slots,
        rows=slots * CAP,
        padded=slots * PAD,
    )
    scratch = scratch_of(c)
    vmem, anywhere = pl.BlockSpec(memory_space=pltpu.VMEM), pl.BlockSpec(memory_space=pl.ANY)
    return pl.pallas_call(
        functools.partial(kernel, c, list(scratch)),
        out_shape=jax.ShapeDtypeStruct(residual.shape, BF16),
        in_specs=[vmem] * 8 + [anywhere] * 4,
        out_specs=vmem,
        scratch_shapes=list(scratch.values()),
        compiler_params=pltpu.CompilerParams(
            collective_id=0, has_side_effects=True, vmem_limit_bytes=56 * 1024 * 1024
        ),
    )(
        queries,
        keys,
        values,
        log_decay,
        residual,
        prenorm_multiplier[None, :],
        picked_unit_indices,
        picked_unit_indices.T,
        out_weight,
        router_weight,
        expert_up_weight,
        down_weight,
    )


def solution(mesh):
    n = mesh.shape["seq"]
    xs = 4 if n % 4 == 0 and n > 4 else 2
    sizes = (n, xs, n // xs, mesh.shape["tp"] // CORES)
    in_specs = (
        P("seq", "tp"),
        P("seq", "tp"),
        P("seq", "tp"),
        P("tp", "seq"),
        P("seq", "tp"),
        P("tp", None),
        P("tp"),
        P(),
        P("seq", None),
        P("seq", None, "tp"),
        P("seq", "tp", None),
    )
    return jax.shard_map(
        functools.partial(body, sizes),
        mesh=mesh,
        in_specs=in_specs,
        out_specs=P("seq", "tp"),
        check_vma=False,
    )
```

time: 555 us -> 123 us (0.22)
  the two profiles are of different devices: /device:TPU:2 before, /device:TPU:32 now
where the time goes in v1:
time: 123 us
  Pallas kernels  117 us (95%)
  local copies, waits for them, and re-layouts  6.44 us (5%)
    pallas_call x1, Pallas kernels, body(): pl.pallas_call(functools.partial(kernel, c, list(scratch)), out_shape=jax...  117 us
    unnamed x3, local copies, waits for them, and re-layouts  5.18 us

profile of v1, /device:TPU:32, one launch (start us, length us, event | category | flops | bytes accessed | tf_op | source)
XLA Modules:
  0.0 123.2 jit_solution(4881013279265975281)
XLA Ops:
  0.0 1.3 %broadcast_in_dim.3.refs_5_ = f32[1,384]{1,0:T(1,128)} reshape(f32[384]{0:T(512)} %param.17) | data formatting | bytes 3072 | tf_op jit(solution)/shard_map/broadcast_in_dim | solution.py:513
  1.3 1.5 %copy.12.refs_6_ = s32[256,2]{1,0:T(8,128)} copy(s32[256,2]{0,1:T(2,128)} %param.19) | data formatting | bytes 4096 | tf_op args[8]
  2.7 2.1 %copy.13.refs_9_ = bf16[3072,32]{1,0:T(8,128)(2,1)} copy(bf16[3072,32]{0,1:T(8,128)(2,1)} %param.18) | data formatting | bytes 393216 | tf_op args[7]
  4.8 116.7 %shard_map.109 = bf16[256,384]{1,0:T(8,128)(2,1)} custom-call(bf16[256,512]{1,0:T(8,128)(2,1)} %refs_0_.1, bf16[256,512]{1,0:T(8,128)(2,1)} %refs_1_.1, bf16[256,512]{1,0:T(8,128)(2,1)} %refs_2_.1, f32[4,256]{1,0:T(4,128)} %refs_3_.1, bf16[256,384]{1,0:T(8,128)(2,1)} %refs_4_.1, f32[1,384]{1,0:T(1,128)} %broadcast_in_dim.3.refs_5_, s32[256,2]{1,0:T(8,128)} %copy.12.refs_6_, ...), custom_call_target="tpu_custom_call" | custom-call | tf_op jit(solution)/shard_map/pallas_call | solution.py:498
  121.6 1.6 %copy.15 = bf16[256,384]{1,0:T(8,128)(2,1)} copy(bf16[256,384]{1,0:T(8,128)(2,1)} %shard_map.109) | data formatting | bytes 393216

commit v2 on v1

v2 whole, which is shorter than its diff:
```python
import functools

import jax
import jax.numpy as jnp
from jax import lax
from jax.experimental import pallas as pl
from jax.experimental.pallas import tpu as pltpu
from jax.sharding import PartitionSpec as P

EPSILON = 1e-05
MESH = pl.DeviceIdType.MESH
F32, BF16 = jnp.float32, jnp.bfloat16
HIGHEST = lax.Precision.HIGHEST
CAP = 24
PAD = 32
CORES = 2


def mm(a, b):
    return jnp.dot(a, b, preferred_element_type=F32)


def mm_nt(a, b):
    return lax.dot_general(a, b, (((1,), (1,)), ((), ())), preferred_element_type=F32)


def mm_tn(a, b):
    return lax.dot_general(a, b, (((0,), (0,)), ((), ())), preferred_element_type=F32)


def iota(shape, dim):
    return lax.broadcasted_iota(jnp.int32, shape, dim)


def flag(mask):
    return jnp.where(mask, 1.0, 0.0).astype(BF16)


def split2(x):
    high = x.astype(BF16)
    return high, (x - high.astype(F32)).astype(BF16)


def to_column(row):
    n = row.shape[1]
    eye = iota((n, n), 0) == iota((n, n), 1)
    return jnp.sum(jnp.where(eye, row, 0.0), axis=1, keepdims=True)


def to_row(column):
    n = column.shape[0]
    eye = iota((n, n), 0) == iota((n, n), 1)
    return jnp.sum(jnp.where(eye, column, 0.0), axis=0, keepdims=True)


def send(src, dst, send_sem, recv_sem, device):
    pltpu.make_async_remote_copy(
        src_ref=src,
        dst_ref=dst,
        send_sem=send_sem,
        recv_sem=recv_sem,
        device_id=device,
        device_id_type=MESH,
    ).start()


def wait(ref, sem):
    pltpu.make_async_copy(ref, ref, sem).wait()


def scratch_of(c):
    n, y, g, w, t, hd = c["n"], c["y"], c["g"], c["w"], c["t"], c["hd"]
    tp, f, rows = y * CORES, c["f"], n * CAP
    dma = pltpu.SemaphoreType.DMA
    return dict(
        owv=pltpu.VMEM((tp, c["a"], w), BF16),
        rwv=pltpu.VMEM((n, w), BF16),
        upv=pltpu.VMEM((y, CORES * w, f), BF16),
        dnv=pltpu.VMEM((y, f, CORES * w), BF16),
        ub=pltpu.VMEM((n, hd, 128), BF16),
        ur=pltpu.VMEM((n, hd, 128), BF16),
        ts=pltpu.VMEM((c["heads"], 1, 128), F32),
        tr=pltpu.VMEM((n, 1, 128), F32),
        sb=pltpu.VMEM((n, hd, 128), BF16),
        se=pltpu.VMEM((n, hd, 128), BF16),
        within=pltpu.VMEM((t, c["a"]), F32),
        ps1=pltpu.VMEM((y, t, w), BF16),
        pr1=pltpu.VMEM((y, t, w), BF16),
        ps2=pltpu.VMEM((y, t, w), BF16),
        pr2=pltpu.VMEM((y, t, w), BF16),
        rl1=pltpu.VMEM((2, t // 2, w), BF16),
        sqs=pltpu.VMEM((1, t), F32),
        sqr=pltpu.VMEM((tp, 1, t), F32),
        fs=pltpu.VMEM((n, 1, 128), F32),
        fr=pltpu.VMEM((n, 1, 128), F32),
        cs=pltpu.VMEM((2, 1, t), F32),
        cr=pltpu.VMEM((tp, 2, 1, t), F32),
        pm=pltpu.VMEM((n * PAD, t), BF16),
        q0=pltpu.VMEM((t, n * PAD), BF16),
        q1=pltpu.VMEM((t, n * PAD), BF16),
        dsp=pltpu.VMEM((n * PAD, w), BF16),
        xr=pltpu.VMEM((n * PAD, w), BF16),
        xg=pltpu.VMEM((y, rows, CORES * w), BF16),
        mb=pltpu.VMEM((y, rows, w), F32),
        ps=pltpu.VMEM((y, rows, w), BF16),
        pr=pltpu.VMEM((y, rows, w), BF16),
        ys=pltpu.VMEM((y, rows, w), BF16),
        yr=pltpu.VMEM((y, rows, w), BF16),
        rl=pltpu.VMEM((rows, w), BF16),
        hs=pltpu.VMEM((n * PAD, w), BF16),
        ret=pltpu.VMEM((n * PAD, w), BF16),
        w_ow=dma((tp,)),
        w_up=dma((y,)),
        w_dn=dma((y,)),
        w_rw=dma((1,)),
        m_s=dma((8,)),
        m_r=dma((8,)),
        p1_s=dma((y,)),
        p1_r=dma((y,)),
        p2_s=dma((y,)),
        p2_r=dma((y,)),
        p3_s=dma((2,)),
        p3_r=dma((2,)),
        l1_s=dma((2,)),
        l1_r=dma((2,)),
        x_s=dma((g,)),
        x_r=dma((g,)),
        a_s=dma((g, y)),
        a_r=dma((g, y)),
        b_s=dma((g, y)),
        b_r=dma((g, y)),
        c_s=dma((g, y)),
        c_r=dma((g, y)),
        d_s=dma((g, y)),
        d_r=dma((g, y)),
        e_s=dma((g, 2)),
        e_r=dma((g, 2)),
        f_s=dma((g, 2)),
        f_r=dma((g, 2)),
        l_s=dma((g, 2)),
        l_r=dma((g, 2)),
        h_s=dma((g,)),
    )


def kernel(c, names, *refs):
    (q, k, v, ld, res, mult, idst, ow, rw, up, dn, out) = refs[:12]
    r = dict(zip(names, refs[12:]))
    n, xs, zs, ys_n, groups = c["n"], c["x"], c["z"], c["y"], c["groups"]
    heads, t, w, hd, tp_n = c["heads"], c["t"], c["w"], c["hd"], c["y"] * CORES
    starts = [xs * sum(len(steps) for steps in groups[:g]) for g in range(len(groups))]
    sizes = [xs * len(steps) for steps in groups]
    s, tp = lax.axis_index("seq"), lax.axis_index("tp")
    z, x = s // xs, lax.rem(s, xs)
    y, core = tp // CORES, lax.rem(tp, CORES)
    partner = (s, y * CORES + 1 - core)
    ahead, behind, opposite = (lax.rem(y + d, ys_n) for d in (1, 3, 2))
    sides = ((ahead, (s, ahead * CORES + core)), (behind, (s, behind * CORES + core)))
    m_s, m_r = r["m_s"], r["m_r"]

    def seq_peers(body):
        def step(i, carry):
            distance = (n - i + 1) // 2
            body(lax.rem(s + jnp.where(lax.rem(i, 2) == 1, distance, n - distance), n))
            return carry

        lax.fori_loop(1, n, step, 0)

    def tp_peers(body):
        def step(i, carry):
            body(lax.rem(tp + i, tp_n))
            return carry

        lax.fori_loop(1, tp_n, step, 0)

    pending = []
    barrier = pltpu.get_barrier_semaphore()
    seq_peers(
        lambda p: pl.semaphore_signal(barrier, inc=1, device_id=(p, tp), device_id_type=MESH)
    )
    tp_peers(lambda p: pl.semaphore_signal(barrier, inc=1, device_id=(s, p), device_id_type=MESH))

    weights = []
    for u in range(tp_n):
        weights.append(
            pltpu.make_async_copy(ow.at[:, pl.ds(u * w, w)], r["owv"].at[u], r["w_ow"].at[u])
        )
    weights.append(
        pltpu.make_async_copy(
            rw.at[:, pl.ds(pl.multiple_of(tp * w, w), w)], r["rwv"], r["w_rw"].at[0]
        )
    )
    for i in range(ys_n):
        part = pl.ds(i * CORES * w, CORES * w)
        weights.append(
            pltpu.make_async_copy(up.at[0, part, :], r["upv"].at[i], r["w_up"].at[i])
        )
    for i in range(ys_n):
        part = pl.ds(i * CORES * w, CORES * w)
        weights.append(
            pltpu.make_async_copy(dn.at[0, :, part], r["dnv"].at[i], r["w_dn"].at[i])
        )
    for copy in weights:
        copy.start()

    logs = ld[...]
    upper = jnp.where(iota((t, t), 0) <= iota((t, t), 1), 1.0, 0.0)
    lower = jnp.where(iota((t, t), 0) >= iota((t, t), 1), 1.0, 0.0)
    c_row = jnp.dot(logs, upper, precision=HIGHEST, preferred_element_type=F32)
    c_col = lax.dot_general(
        lower, logs, (((1,), (1,)), ((), ())), precision=HIGHEST, preferred_element_type=F32
    )
    per_head = 128 // hd
    for h in range(heads):
        head = pl.ds(h * 128, 128)
        total = c_row[h : h + 1, t - 1 : t]
        r["ts"][h] = jnp.broadcast_to(total, (1, 128))
        weighted = k[:, head].astype(F32) * jnp.exp(total - c_col[:, h : h + 1])
        high, low = split2(weighted)
        product = (mm_tn(high, v[:, head]) + mm_tn(low, v[:, head])).astype(BF16)
        for i in range(per_head):
            r["ub"][h * per_head + i] = product[i * hd : (i + 1) * hd]

    pl.semaphore_wait(barrier, n - 1 + tp_n - 1)

    ub, ur, ts, tr, sb, se = (r[name] for name in ("ub", "ur", "ts", "tr", "sb", "se"))
    seq_peers(lambda p: send(ts.at[p // per_head], tr.at[s], m_s.at[0], m_r.at[0], (p, tp)))
    seq_peers(lambda p: send(ub.at[p], ur.at[s], m_s.at[1], m_r.at[1], (p, tp)))
    pending.append((tr.at[pl.ds(0, n - 1)], m_s.at[0]))
    pending.append((ur.at[pl.ds(0, n - 1)], m_s.at[1]))
    tr[s] = ts[s // per_head]
    ur[s] = ub[s]

    ids_r = idst[...]
    first, second = (to_column(ids_r[j : j + 1, :].astype(F32)) for j in range(2))
    picks = (first, second)
    names_lane = iota((t, n), 1).astype(F32)
    slots_c = []
    before = flag(iota((t, t), 1) < iota((t, t), 0))
    counts = mm(before, flag((first == names_lane) | (second == names_lane)))
    for j, pick, q_ref in ((0, first, r["q0"]), (1, second, r["q1"])):
        slot = jnp.sum(jnp.where(pick == names_lane, counts, 0.0), axis=1, keepdims=True)
        slots_c.append(slot)
        target = pick * PAD + slot
        q_ref[...] = flag(iota((t, n * PAD), 1).astype(F32) == target)
    first, second = ids_r[0:1, :], ids_r[1:2, :]
    names_sub = iota((n, t), 0)
    after = flag(iota((t, t), 0) < iota((t, t), 1))
    counts = mm(flag((first == names_sub) | (second == names_sub)), after)
    targets = []
    for pick in (first, second):
        slot = jnp.sum(jnp.where(pick == names_sub, counts, 0.0), axis=0, keepdims=True)
        targets.append(pick.astype(F32) * PAD + slot)
    place = iota((n * PAD, t), 0).astype(F32)
    r["pm"][...] = flag((place == targets[0]) | (place == targets[1]))

    causal = iota((t, t), 0) >= iota((t, t), 1)
    for h in range(heads):
        head = pl.ds(h * 128, 128)
        scores = mm_nt(q[:, head], k[:, head])
        gap = jnp.where(causal, c_col[:, h : h + 1] - c_row[h : h + 1, :], 0.0)
        intra = jnp.where(causal, scores * jnp.exp(gap), 0.0).astype(BF16)
        r["within"][:, head] = mm(intra, v[:, head])

    wait(tr.at[pl.ds(0, n - 1)], m_r.at[0])
    wait(ur.at[pl.ds(0, n - 1)], m_r.at[1])

    def scan(b, state):
        sb[b] = state.astype(BF16)
        return jnp.exp(tr[b]) * state + ur[b].astype(F32)

    lax.fori_loop(0, n, scan, jnp.zeros((hd, 128), F32))
    seq_peers(lambda p: send(sb.at[p], se.at[s], m_s.at[2], m_r.at[2], (p, tp)))
    pending.append((se.at[pl.ds(0, n - 1)], m_s.at[2]))
    se[s] = sb[s]
    wait(se.at[pl.ds(0, n - 1)], m_r.at[2])

    attended = []
    for h in range(heads):
        head = pl.ds(h * 128, 128)
        state = se[h * per_head : (h + 1) * per_head].reshape(128, 128)
        head_out = r["within"][:, head] + mm(q[:, head], state) * jnp.exp(c_col[:, h : h + 1])
        mean = jnp.mean(head_out * head_out, axis=1, keepdims=True)
        attended.append((head_out * lax.rsqrt(mean + EPSILON)).astype(BF16))
    attention = jnp.concatenate(attended, axis=1)

    ps1, pr1, ps2, pr2 = (r[name] for name in ("ps1", "pr1", "ps2", "pr2"))
    for copy in weights[: tp_n + 1]:
        copy.wait()
    for to in (opposite, ahead, behind, y):
        ps1[to] = mm(attention, r["owv"][to * CORES + 1 - core]).astype(BF16)
        send(ps1.at[to], pr1.at[to], r["p1_s"].at[to], r["p1_r"].at[to], partner)
        pending.append((ps1.at[to], r["p1_s"].at[to]))

    def chip_sum(to):
        mine = mm(attention, r["owv"][to * CORES + core])
        wait(pr1.at[to], r["p1_r"].at[to])
        return mine + pr1[to].astype(F32)

    rl1 = r["rl1"]
    halves = (pl.ds(0, t // 2), pl.ds(t // 2, t // 2))
    ps2[2] = chip_sum(opposite).astype(BF16)
    for i, (_, device) in enumerate(sides):
        send(ps2.at[2, halves[i]], rl1.at[i], r["l1_s"].at[i], r["l1_r"].at[i], device)
        pending.append((rl1.at[i], r["l1_s"].at[i]))
    with_relay = []
    for i, (to, device) in enumerate(sides):
        mine = chip_sum(to)
        ps2[i, halves[1 - i]] = mine[(1 - i) * (t // 2) : (2 - i) * (t // 2)].astype(BF16)
        piece = (i, halves[1 - i])
        send(ps2.at[piece], pr2.at[piece], r["p3_s"].at[i], r["p3_r"].at[i], device)
        pending.append((ps2.at[piece], r["p3_s"].at[i]))
        with_relay.append(mine[i * (t // 2) : (i + 1) * (t // 2)])
    for i, (_, device) in enumerate(sides):
        wait(rl1.at[i], r["l1_r"].at[i])
        piece = (i, halves[i])
        ps2[piece] = (with_relay[i] + rl1[i].astype(F32)).astype(BF16)
        send(ps2.at[piece], pr2.at[piece], r["p2_s"].at[i], r["p2_r"].at[i], device)
        pending.append((ps2.at[piece], r["p2_s"].at[i]))
    hidden = res[...].astype(F32) + chip_sum(y)
    for i in range(2):
        wait(pr2.at[i, halves[1 - i]], r["p3_r"].at[i])
        wait(pr2.at[i, halves[i]], r["p2_r"].at[i])
        hidden = hidden + pr2[i].astype(F32)

    dsp, xr, ret = r["dsp"], r["xr"], r["ret"]
    scaled = (hidden * mult[...][None, :]).astype(BF16)
    dsp[...] = mm(r["pm"][...], scaled).astype(BF16)

    def rows_of(index):
        return pl.ds(pl.multiple_of(index * PAD, PAD), PAD)

    home_group = [g for g, steps in enumerate(groups) if steps[0] == 0][0]
    home_slot = starts[home_group]

    def group_peers(g, sign, body):
        def step(j, carry):
            dz = groups[g][0]
            for i in range(1, len(groups[g])):
                dz = jnp.where(j < i * xs, dz, groups[g][i])
            dx = lax.rem(j, xs)
            pz = lax.rem(z + zs + sign * dz, zs)
            px = lax.rem(x + xs + sign * dx, xs)
            body(starts[g] + j, pz * xs + px)
            return carry

        lax.fori_loop(0 if g != home_group else 1, sizes[g], step, 0)

    for g in range(len(groups)):
        group_peers(
            g,
            1,
            lambda j, p, g=g: send(
                dsp.at[rows_of(p)], xr.at[rows_of(j)], r["x_s"].at[g], r["x_r"].at[g], (p, tp)
            ),
        )
    def group_ref(g):
        skip = 1 if g == home_group else 0
        return xr.at[pl.ds((starts[g] + skip) * PAD, (sizes[g] - skip) * PAD)]

    for g in range(len(groups)):
        pending.append((group_ref(g), r["x_s"].at[g]))
    xr[home_slot * PAD : (home_slot + 1) * PAD] = dsp[rows_of(s)]

    sqs, sqr = r["sqs"], r["sqr"]
    high, low = split2(hidden * hidden)
    ones = jnp.ones((8, w), BF16)
    sqs[...] = (mm_nt(ones, high) + mm_nt(ones, low))[0:1]
    tp_peers(lambda p: send(sqs, sqr.at[tp], m_s.at[3], m_r.at[3], (s, p)))
    pending.append((sqr.at[pl.ds(0, tp_n - 1)], m_s.at[3]))
    sqr[tp] = sqs[...]
    partial_logits = mm_nt(scaled, r["rwv"][...])
    wait(sqr.at[pl.ds(0, tp_n - 1)], m_r.at[3])
    square_sum = sqr[0]
    for u in range(1, tp_n):
        square_sum = square_sum + sqr[u]
    inverse = to_column(lax.rsqrt(square_sum / (w * tp_n) + EPSILON))
    factors = jnp.zeros((n, 128), F32)
    lane = iota((t, 128), 1).astype(F32)
    for pick, slot in zip(picks, slots_c):
        chosen = flag(pick == names_lane)
        rest = jnp.where(slot == lane, inverse, 0.0)
        for _ in range(3):
            piece = rest.astype(BF16)
            rest = rest - piece.astype(F32)
            factors = factors + mm_tn(chosen, piece)
    fs, fr = r["fs"], r["fr"]
    for i in range(n):
        fs[i] = factors[i : i + 1]
    for g in range(len(groups)):
        group_peers(
            g,
            1,
            lambda j, p, g=g: send(
                fs.at[p], fr.at[j], m_s.at[6], m_r.at[6], (p, tp)
            ),
        )
    pending.append((fr.at[pl.ds(0, n - 1)], m_s.at[6]))
    fr[home_slot] = fs[s]

    cs, cr = r["cs"], r["cr"]
    logits = partial_logits * inverse
    for j in range(2):
        chosen = jnp.where(picks[j] == names_lane, logits, 0.0)
        cs[j] = to_row(jnp.sum(chosen, axis=1, keepdims=True))
    tp_peers(lambda p: send(cs, cr.at[tp], m_s.at[4], m_r.at[4], (s, p)))
    pending.append((cr.at[pl.ds(0, tp_n - 1)], m_s.at[4]))
    cr[tp] = cs[...]

    xg, mb, ps, pr = (r[name] for name in ("xg", "mb", "ps", "pr"))
    ys, yr, rl, hs = (r[name] for name in ("ys", "yr", "rl", "hs"))

    def compaction(count):
        row, lane = iota((count * CAP, count * PAD), 0), iota((count * CAP, count * PAD), 1)
        block = (row * 2731) >> 16
        return flag(lane == block * PAD + (row - block * CAP))

    def expansion(count):
        row, lane = iota((count * PAD, count * CAP), 0), iota((count * PAD, count * CAP), 1)
        block = (lane * 2731) >> 16
        return flag(row == block * PAD + (lane - block * CAP))

    def slots_of(g, unit):
        return pl.ds(starts[g] * unit, sizes[g] * unit)

    def rows_in(g):
        return slots_of(g, CAP)

    def half_rows(g, i):
        return pl.ds(starts[g] * CAP + i * sizes[g] * CAP // 2, sizes[g] * CAP // 2)

    own_half = pl.ds(pl.multiple_of(core * w, w), w)
    other_half = pl.ds(pl.multiple_of((1 - core) * w, w), w)
    origins = (behind, ahead)

    def spread_out(g):
        wait(group_ref(g), r["x_r"].at[g])
        packed = mm(compaction(sizes[g]), xr[slots_of(g, PAD)]).astype(BF16)
        for side in range(CORES):

            @pl.when(core == side)
            def _(side=side):
                xg[y, rows_in(g), side * w : (side + 1) * w] = packed

        piece = xg.at[y, rows_in(g), own_half]
        for i, (_, device) in enumerate(sides):
            send(piece, piece, r["a_s"].at[g, i], r["a_r"].at[g, i], device)
            pending.append((piece, r["a_s"].at[g, i]))
        send(piece, piece, r["b_s"].at[g, y], r["b_r"].at[g, y], partner)
        pending.append((piece, r["b_s"].at[g, y]))

    def pass_over(g, block):
        piece = xg.at[block, rows_in(g), own_half]
        send(piece, piece, r["b_s"].at[g, block], r["b_r"].at[g, block], partner)
        pending.append((piece, r["b_s"].at[g, block]))

    def pass_on(g):
        for i, (_, device) in enumerate(sides):
            wait(xg.at[origins[i], rows_in(g), own_half], r["a_r"].at[g, i])
            piece = xg.at[origins[i], half_rows(g, i), own_half]
            send(piece, piece, r["f_s"].at[g, i], r["f_r"].at[g, i], device)
            pending.append((piece, r["f_s"].at[g, i]))
            pass_over(g, origins[i])

    def pass_far(g):
        for i in range(2):
            wait(xg.at[opposite, half_rows(g, i), own_half], r["f_r"].at[g, i])
        pass_over(g, opposite)

    waited = []

    def expert(g):
        for i in range(ys_n):
            wait(xg.at[i, rows_in(g), other_half], r["b_r"].at[g, i])
        total = mm(xg[0, rows_in(g)], r["upv"][0])
        for i in range(1, ys_n):
            total = total + mm(xg[i, rows_in(g)], r["upv"][i])
        if not waited:
            wait(fr.at[pl.ds(0, n - 1)], m_r.at[6])
            waited.append(g)
        mine = range(starts[g], starts[g] + sizes[g])
        spots = [jnp.broadcast_to(fr[j], (CAP, 128)) for j in mine]
        spots = jnp.concatenate(spots, axis=0)
        spot_row, spot_lane = iota((sizes[g] * CAP, 128), 0), iota((sizes[g] * CAP, 128), 1)
        spot_row = spot_row - ((spot_row * 2731) >> 16) * CAP
        total = total * jnp.sum(jnp.where(spot_lane == spot_row, spots, 0.0), axis=1, keepdims=True)
        hidden_rows = (total / (1.0 + jnp.exp(-total))).astype(BF16)
        for i in range(ys_n):
            part = mm(hidden_rows, r["dnv"][i])
            left, right = part[:, :w], part[:, w:]
            mb[i, rows_in(g)] = jnp.where(core == 0, left, right)
            ps[i, rows_in(g)] = jnp.where(core == 0, right, left).astype(BF16)
            piece = (i, rows_in(g))
            send(ps.at[piece], pr.at[piece], r["c_s"].at[g, i], r["c_r"].at[g, i], partner)
            pending.append((ps.at[piece], r["c_s"].at[g, i]))

    def chip_rows(g, to, part):
        return mb[to, part] + pr[to, part].astype(F32)

    def sum_far(g):
        for i in range(ys_n):
            wait(pr.at[i, rows_in(g)], r["c_r"].at[g, i])
        for i, (_, device) in enumerate(sides):
            part = half_rows(g, i)
            ys[2, part] = chip_rows(g, opposite, part).astype(BF16)
            send(ys.at[2, part], rl.at[part], r["l_s"].at[g, i], r["l_r"].at[g, i], device)
            pending.append((ys.at[2, part], r["l_s"].at[g, i]))
        for i, (to, device) in enumerate(sides):
            part = half_rows(g, 1 - i)
            ys[i, part] = chip_rows(g, to, part).astype(BF16)
            send(ys.at[i, part], yr.at[i, part], r["e_s"].at[g, i], r["e_r"].at[g, i], device)
            pending.append((ys.at[i, part], r["e_s"].at[g, i]))

    def sum_near(g):
        for i, (to, device) in enumerate(sides):
            part = half_rows(g, i)
            wait(rl.at[part], r["l_r"].at[g, i])
            ys[i, part] = (chip_rows(g, to, part) + rl[part].astype(F32)).astype(BF16)
            send(ys.at[i, part], yr.at[i, part], r["d_s"].at[g, i], r["d_r"].at[g, i], device)
            pending.append((ys.at[i, part], r["d_s"].at[g, i]))

    def home(g):
        total = chip_rows(g, y, rows_in(g))
        for i in range(2):
            wait(yr.at[i, half_rows(g, 1 - i)], r["e_r"].at[g, i])
            wait(yr.at[i, half_rows(g, i)], r["d_r"].at[g, i])
            total = total + yr[i, rows_in(g)].astype(F32)
        hs[slots_of(g, PAD)] = mm(expansion(sizes[g]), total.astype(BF16)).astype(BF16)
        group_peers(
            g,
            -1,
            lambda j, p: send(
                hs.at[rows_of(j)], ret.at[rows_of(s)], r["h_s"].at[g], m_r.at[5], (p, tp)
            ),
        )
        pending.append((group_ref(g), r["h_s"].at[g]))
        if g == home_group:
            ret[rows_of(s)] = hs[home_slot * PAD : (home_slot + 1) * PAD]

    for copy in weights[tp_n + 1 :]:
        copy.wait()
    stages = (spread_out, pass_on, pass_far, expert, sum_far, sum_near, home)
    todo = {g: list(stages) for g in range(len(groups))}
    for g in c["order"]:
        todo[g].pop(0)(g)

    wait(cr.at[pl.ds(0, tp_n - 1)], m_r.at[4])
    gates = []
    for j in range(2):
        logit = cr[0, j]
        for u in range(1, tp_n):
            logit = logit + cr[u, j]
        gates.append(jax.nn.sigmoid(logit))
    both = gates[0] + gates[1]
    shares = [to_column(gate / both) for gate in gates]
    wait(ret.at[pl.ds(0, (n - 1) * PAD)], m_r.at[5])
    returned = ret[...]
    mix = shares[0] * mm(r["q0"][...], returned) + shares[1] * mm(r["q1"][...], returned)
    out[...] = (hidden + mix).astype(BF16)

    for ref, sem in pending:
        wait(ref, sem)


GROUPS = {8: [(1, 7), (2, 6), (3, 5), (0, 4)]}
ORDERS = {8: [0, 1, 0, 1, 2, 0, 3, 0, 2, 0, 1, 1, 2, 3, 1, 2, 0, 1, 3, 2, 3, 0, 1, 2, 3, 2, 3, 3]}


def stepped(count, stages=7):
    return [
        step - lag
        for step in range(count + stages - 1)
        for lag in range(stages)
        if 0 <= step - lag < count
    ]


def body(
    sizes,
    queries,
    keys,
    values,
    log_decay,
    residual,
    out_weight,
    prenorm_multiplier,
    router_weight,
    picked_unit_indices,
    expert_up_weight,
    down_weight,
):
    n, xs, zs, ys = sizes
    half = zs // 2
    groups = GROUPS.get(zs) or [(d, zs - d) for d in range(1, half)] + [(0, half)]
    order = ORDERS.get(zs) or stepped(len(groups))
    heads = log_decay.shape[0]
    c = dict(
        n=n,
        x=xs,
        z=zs,
        y=ys,
        groups=groups,
        order=order,
        g=len(groups),
        heads=heads,
        t=queries.shape[0],
        a=queries.shape[1],
        w=residual.shape[1],
        f=expert_up_weight.shape[2],
        hd=heads * 128 // n,
    )
    scratch = scratch_of(c)
    vmem, anywhere = pl.BlockSpec(memory_space=pltpu.VMEM), pl.BlockSpec(memory_space=pl.ANY)
    return pl.pallas_call(
        functools.partial(kernel, c, list(scratch)),
        out_shape=jax.ShapeDtypeStruct(residual.shape, BF16),
        in_specs=[vmem] * 7 + [anywhere] * 4,
        out_specs=vmem,
        scratch_shapes=list(scratch.values()),
        compiler_params=pltpu.CompilerParams(
            collective_id=0, has_side_effects=True, vmem_limit_bytes=56 * 1024 * 1024
        ),
    )(
        queries,
        keys,
        values,
        log_decay,
        residual,
        prenorm_multiplier,
        picked_unit_indices.T,
        out_weight,
        router_weight.T,
        expert_up_weight,
        down_weight,
    )


def solution(mesh):
    n = mesh.shape["seq"]
    xs = 4 if n % 4 == 0 and n > 4 else 2
    sizes = (n, xs, n // xs, mesh.shape["tp"] // CORES)
    in_specs = (
        P("seq", "tp"),
        P("seq", "tp"),
        P("seq", "tp"),
        P("tp", "seq"),
        P("seq", "tp"),
        P("tp", None),
        P("tp"),
        P(),
        P("seq", None),
        P("seq", None, "tp"),
        P("seq", "tp", None),
    )
    return jax.shard_map(
        functools.partial(body, sizes),
        mesh=mesh,
        in_specs=in_specs,
        out_specs=P("seq", "tp"),
        check_vma=False,
    )
```

time: 123 us -> 104 us (0.85)
  the two profiles are of different devices: /device:TPU:32 before, /device:TPU:2 now
where the time goes in v2:
time: 104 us; the launch traced here: 103 us
  Pallas kernels  101 us (97%)
  local copies, waits for them, and re-layouts  1.62 us (2%)
    pallas_call x1, Pallas kernels, body(): pl.pallas_call(functools.partial(kernel, c, list(scratch)), out_shape=jax...  101 us

profile of v2, /device:TPU:2, one launch (start us, length us, event | category | flops | bytes accessed | tf_op | source)
XLA Modules:
  0.0 103.1 jit_solution(6556264716855497273)
XLA Ops:
  0.0 101.5 %shard_map.109 = bf16[256,384]{1,0:T(8,128)(2,1)} custom-call(bf16[256,512]{1,0:T(8,128)(2,1)} %refs_0_.1, bf16[256,512]{1,0:T(8,128)(2,1)} %refs_1_.1, bf16[256,512]{1,0:T(8,128)(2,1)} %refs_2_.1, f32[4,256]{1,0:T(4,128)} %refs_3_.1, bf16[256,384]{1,0:T(8,128)(2,1)} %refs_4_.1, f32[384]{0:T(512)} %refs_5_.1, s32[2,256]{1,0:T(2,128)} %bitcast.3, ...), custom_call_target="tpu_custom_call" | custom-call | tf_op jit(solution)/shard_map/pallas_call | solution.py:614
  101.5 1.6 %copy.13 = bf16[256,384]{1,0:T(8,128)(2,1)} copy(bf16[256,384]{1,0:T(8,128)(2,1)} %shard_map.109) | data formatting | bytes 393216

commit v3 on v2

--- a/solution.py
+++ b/solution.py
@@ -12,7 +12,8 @@
 F32, BF16 = jnp.float32, jnp.bfloat16
 HIGHEST = lax.Precision.HIGHEST
 CAP = 24
-PAD = 32
+TILE = 16
+PIECES = 5
 CORES = 2
 
 
@@ -51,6 +52,33 @@
     n = column.shape[0]
     eye = iota((n, n), 0) == iota((n, n), 1)
     return jnp.sum(jnp.where(eye, column, 0.0), axis=0, keepdims=True)
+
+
+def places(block, slot):
+    late = slot >= TILE
+    base = block * TILE + slot
+    nowhere = jnp.full(base.shape, -1, base.dtype)
+    return (
+        jnp.where(late, nowhere, base),
+        jnp.where(late, base - TILE, nowhere),
+        jnp.where(late, base - TILE // 2, nowhere),
+    )
+
+
+def to_pieces(parts, rows, out, where):
+    head = mm(parts[0], rows).astype(BF16)
+    for i in range(3):
+        out[i, where] = head[:, i * 128 : (i + 1) * 128]
+    tail = mm(parts[1], rows[:, 0:128]) + mm(parts[2], rows[:, 128:256])
+    out[3, where] = tail.astype(BF16)
+    out[4, where] = mm(parts[1], rows[:, 256:384]).astype(BF16)
+
+
+def from_pieces(parts, pieces, where):
+    head = jnp.concatenate([pieces[i, where] for i in range(3)], axis=1)
+    third, fourth = pieces[3, where], pieces[4, where]
+    tail = [mm(parts[1], third), mm(parts[2], third), mm(parts[1], fourth)]
+    return mm(parts[0], head) + jnp.concatenate(tail, axis=1)
 
 
 def send(src, dst, send_sem, recv_sem, device):
@@ -95,20 +123,19 @@
         fr=pltpu.VMEM((n, 1, 128), F32),
         cs=pltpu.VMEM((2, 1, t), F32),
         cr=pltpu.VMEM((tp, 2, 1, t), F32),
-        pm=pltpu.VMEM((n * PAD, t), BF16),
-        q0=pltpu.VMEM((t, n * PAD), BF16),
-        q1=pltpu.VMEM((t, n * PAD), BF16),
-        dsp=pltpu.VMEM((n * PAD, w), BF16),
-        xr=pltpu.VMEM((n * PAD, w), BF16),
-        xg=pltpu.VMEM((y, rows, CORES * w), BF16),
+        pm=pltpu.VMEM((3, n * TILE, t), BF16),
+        q=pltpu.VMEM((2, 3, t, n * TILE), BF16),
+        dsp=pltpu.VMEM((PIECES, n * TILE, 128), BF16),
+        xr=pltpu.VMEM((PIECES, n * TILE, 128), BF16),
+        xg=pltpu.VMEM((tp, rows, w), BF16),
         mb=pltpu.VMEM((y, rows, w), F32),
         ps=pltpu.VMEM((y, rows, w), BF16),
         pr=pltpu.VMEM((y, rows, w), BF16),
         ys=pltpu.VMEM((y, rows, w), BF16),
         yr=pltpu.VMEM((y, rows, w), BF16),
         rl=pltpu.VMEM((rows, w), BF16),
-        hs=pltpu.VMEM((n * PAD, w), BF16),
-        ret=pltpu.VMEM((n * PAD, w), BF16),
+        hs=pltpu.VMEM((PIECES, n * TILE, 128), BF16),
+        ret=pltpu.VMEM((PIECES, n * TILE, 128), BF16),
         w_ow=dma((tp,)),
         w_up=dma((y,)),
         w_dn=dma((y,)),
@@ -238,11 +265,11 @@
     slots_c = []
     before = flag(iota((t, t), 1) < iota((t, t), 0))
     counts = mm(before, flag((first == names_lane) | (second == names_lane)))
-    for j, pick, q_ref in ((0, first, r["q0"]), (1, second, r["q1"])):
+    for j, pick in enumerate(picks):
         slot = jnp.sum(jnp.where(pick == names_lane, counts, 0.0), axis=1, keepdims=True)
         slots_c.append(slot)
-        target = pick * PAD + slot
-        q_ref[...] = flag(iota((t, n * PAD), 1).astype(F32) == target)
+        for i, target in enumerate(places(pick, slot)):
+            r["q"][j, i] = flag(iota((t, n * TILE), 1).astype(F32) == target)
     first, second = ids_r[0:1, :], ids_r[1:2, :]
     names_sub = iota((n, t), 0)
     after = flag(iota((t, t), 0) < iota((t, t), 1))
@@ -250,9 +277,10 @@
     targets = []
     for pick in (first, second):
         slot = jnp.sum(jnp.where(pick == names_sub, counts, 0.0), axis=0, keepdims=True)
-        targets.append(pick.astype(F32) * PAD + slot)
-    place = iota((n * PAD, t), 0).astype(F32)
-    r["pm"][...] = flag((place == targets[0]) | (place == targets[1]))
+        targets.append(places(pick.astype(F32), slot))
+    place = iota((n * TILE, t), 0).astype(F32)
+    for i in range(3):
+        r["pm"][i] = flag((place == targets[0][i]) | (place == targets[1][i]))
 
     causal = iota((t, t), 0) >= iota((t, t), 1)
     for h in range(heads):
@@ -325,10 +353,10 @@
 
     dsp, xr, ret = r["dsp"], r["xr"], r["ret"]
     scaled = (hidden * mult[...][None, :]).astype(BF16)
-    dsp[...] = mm(r["pm"][...], scaled).astype(BF16)
+    to_pieces([r["pm"][i] for i in range(3)], scaled, dsp, pl.ds(0, n * TILE))
 
     def rows_of(index):
-        return pl.ds(pl.multiple_of(index * PAD, PAD), PAD)
+        return pl.ds(pl.multiple_of(index * TILE, TILE), TILE)
 
     home_group = [g for g, steps in enumerate(groups) if steps[0] == 0][0]
     home_slot = starts[home_group]
@@ -351,16 +379,16 @@
             g,
             1,
             lambda j, p, g=g: send(
-                dsp.at[rows_of(p)], xr.at[rows_of(j)], r["x_s"].at[g], r["x_r"].at[g], (p, tp)
+                dsp.at[:, rows_of(p)], xr.at[:, rows_of(j)], r["x_s"].at[g], r["x_r"].at[g], (p, tp)
             ),
         )
     def group_ref(g):
         skip = 1 if g == home_group else 0
-        return xr.at[pl.ds((starts[g] + skip) * PAD, (sizes[g] - skip) * PAD)]
+        return xr.at[:, pl.ds((starts[g] + skip) * TILE, (sizes[g] - skip) * TILE)]
 
     for g in range(len(groups)):
         pending.append((group_ref(g), r["x_s"].at[g]))
-    xr[home_slot * PAD : (home_slot + 1) * PAD] = dsp[rows_of(s)]
+    xr[:, home_slot * TILE : (home_slot + 1) * TILE] = dsp[:, rows_of(s)]
 
     sqs, sqr = r["sqs"], r["sqr"]
     high, low = split2(hidden * hidden)
@@ -411,14 +439,14 @@
     ys, yr, rl, hs = (r[name] for name in ("ys", "yr", "rl", "hs"))
 
     def compaction(count):
-        row, lane = iota((count * CAP, count * PAD), 0), iota((count * CAP, count * PAD), 1)
+        row, lane = iota((count * CAP, count * TILE), 0), iota((count * CAP, count * TILE), 1)
         block = (row * 2731) >> 16
-        return flag(lane == block * PAD + (row - block * CAP))
+        return [flag(lane == place) for place in places(block, row - block * CAP)]
 
     def expansion(count):
-        row, lane = iota((count * PAD, count * CAP), 0), iota((count * PAD, count * CAP), 1)
+        row, lane = iota((count * TILE, count * CAP), 0), iota((count * TILE, count * CAP), 1)
         block = (lane * 2731) >> 16
-        return flag(row == block * PAD + (lane - block * CAP))
+        return [flag(row == place) for place in places(block, lane - block * CAP)]
 
     def slots_of(g, unit):
         return pl.ds(starts[g] * unit, sizes[g] * unit)
@@ -429,52 +457,54 @@
     def half_rows(g, i):
         return pl.ds(starts[g] * CAP + i * sizes[g] * CAP // 2, sizes[g] * CAP // 2)
 
-    own_half = pl.ds(pl.multiple_of(core * w, w), w)
-    other_half = pl.ds(pl.multiple_of((1 - core) * w, w), w)
     origins = (behind, ahead)
 
     def spread_out(g):
         wait(group_ref(g), r["x_r"].at[g])
-        packed = mm(compaction(sizes[g]), xr[slots_of(g, PAD)]).astype(BF16)
-        for side in range(CORES):
-
-            @pl.when(core == side)
-            def _(side=side):
-                xg[y, rows_in(g), side * w : (side + 1) * w] = packed
-
-        piece = xg.at[y, rows_in(g), own_half]
+        packed = from_pieces(compaction(sizes[g]), xr, slots_of(g, TILE)).astype(BF16)
+        xg[tp, rows_in(g)] = packed
+        piece = xg.at[tp, rows_in(g)]
         for i, (_, device) in enumerate(sides):
             send(piece, piece, r["a_s"].at[g, i], r["a_r"].at[g, i], device)
             pending.append((piece, r["a_s"].at[g, i]))
+        if g in c["direct"]:
+            across = (s, opposite * CORES + core)
+            send(piece, piece, r["a_s"].at[g, 2], r["a_r"].at[g, 2], across)
+            pending.append((piece, r["a_s"].at[g, 2]))
         send(piece, piece, r["b_s"].at[g, y], r["b_r"].at[g, y], partner)
         pending.append((piece, r["b_s"].at[g, y]))
 
     def pass_over(g, block):
-        piece = xg.at[block, rows_in(g), own_half]
+        piece = xg.at[block * CORES + core, rows_in(g)]
         send(piece, piece, r["b_s"].at[g, block], r["b_r"].at[g, block], partner)
         pending.append((piece, r["b_s"].at[g, block]))
 
     def pass_on(g):
         for i, (_, device) in enumerate(sides):
-            wait(xg.at[origins[i], rows_in(g), own_half], r["a_r"].at[g, i])
-            piece = xg.at[origins[i], half_rows(g, i), own_half]
-            send(piece, piece, r["f_s"].at[g, i], r["f_r"].at[g, i], device)
-            pending.append((piece, r["f_s"].at[g, i]))
+            wait(xg.at[origins[i] * CORES + core, rows_in(g)], r["a_r"].at[g, i])
+            if g not in c["direct"]:
+                piece = xg.at[origins[i] * CORES + core, half_rows(g, i)]
+                send(piece, piece, r["f_s"].at[g, i], r["f_r"].at[g, i], device)
+                pending.append((piece, r["f_s"].at[g, i]))
             pass_over(g, origins[i])
 
     def pass_far(g):
-        for i in range(2):
-            wait(xg.at[opposite, half_rows(g, i), own_half], r["f_r"].at[g, i])
+        if g in c["direct"]:
+            wait(xg.at[opposite * CORES + core, rows_in(g)], r["a_r"].at[g, 2])
+        else:
+            for i in range(2):
+                wait(xg.at[opposite * CORES + core, half_rows(g, i)], r["f_r"].at[g, i])
         pass_over(g, opposite)
 
     waited = []
 
     def expert(g):
         for i in range(ys_n):
-            wait(xg.at[i, rows_in(g), other_half], r["b_r"].at[g, i])
-        total = mm(xg[0, rows_in(g)], r["upv"][0])
-        for i in range(1, ys_n):
-            total = total + mm(xg[i, rows_in(g)], r["upv"][i])
+            wait(xg.at[i * CORES + 1 - core, rows_in(g)], r["b_r"].at[g, i])
+        total = jnp.zeros((sizes[g] * CAP, c["f"]), F32)
+        for i in range(ys_n):
+            both = [xg[i * CORES + side, rows_in(g)] for side in range(CORES)]
+            total = total + mm(jnp.concatenate(both, axis=1), r["upv"][i])
         if not waited:
             wait(fr.at[pl.ds(0, n - 1)], m_r.at[6])
             waited.append(g)
@@ -525,17 +555,17 @@
             wait(yr.at[i, half_rows(g, 1 - i)], r["e_r"].at[g, i])
             wait(yr.at[i, half_rows(g, i)], r["d_r"].at[g, i])
             total = total + yr[i, rows_in(g)].astype(F32)
-        hs[slots_of(g, PAD)] = mm(expansion(sizes[g]), total.astype(BF16)).astype(BF16)
+        to_pieces(expansion(sizes[g]), total.astype(BF16), hs, slots_of(g, TILE))
         group_peers(
             g,
             -1,
             lambda j, p: send(
-                hs.at[rows_of(j)], ret.at[rows_of(s)], r["h_s"].at[g], m_r.at[5], (p, tp)
+                hs.at[:, rows_of(j)], ret.at[:, rows_of(s)], r["h_s"].at[g], m_r.at[5], (p, tp)
             ),
         )
         pending.append((group_ref(g), r["h_s"].at[g]))
         if g == home_group:
-            ret[rows_of(s)] = hs[home_slot * PAD : (home_slot + 1) * PAD]
+            ret[:, rows_of(s)] = hs[:, home_slot * TILE : (home_slot + 1) * TILE]
 
     for copy in weights[tp_n + 1 :]:
         copy.wait()
@@ -553,17 +583,20 @@
         gates.append(jax.nn.sigmoid(logit))
     both = gates[0] + gates[1]
     shares = [to_column(gate / both) for gate in gates]
-    wait(ret.at[pl.ds(0, (n - 1) * PAD)], m_r.at[5])
-    returned = ret[...]
-    mix = shares[0] * mm(r["q0"][...], returned) + shares[1] * mm(r["q1"][...], returned)
-    out[...] = (hidden + mix).astype(BF16)
+    wait(ret.at[:, pl.ds(0, (n - 1) * TILE)], m_r.at[5])
+    mixed = hidden
+    for j in range(2):
+        parts = [r["q"][j, i] for i in range(3)]
+        mixed = mixed + shares[j] * from_pieces(parts, ret, pl.ds(0, n * TILE))
+    out[...] = mixed.astype(BF16)
 
     for ref, sem in pending:
         wait(ref, sem)
 
 
+DIRECT = {8: ()}
 GROUPS = {8: [(1, 7), (2, 6), (3, 5), (0, 4)]}
-ORDERS = {8: [0, 1, 0, 1, 2, 0, 3, 0, 2, 0, 1, 1, 2, 3, 1, 2, 0, 1, 3, 2, 3, 0, 1, 2, 3, 2, 3, 3]}
+ORDERS = {8: [0, 1, 0, 2, 0, 1, 3, 0, 2, 1, 0, 1, 3, 1, 2, 2, 0, 2, 3, 3, 1, 2, 0, 3, 1, 2, 3, 3]}
 
 
 def stepped(count, stages=7):
@@ -601,6 +634,7 @@
         y=ys,
         groups=groups,
         order=order,
+        direct=DIRECT.get(zs, ()),
         g=len(groups),
         heads=heads,
         t=queries.shape[0],

time: 104 us -> 101 us (0.971); the launches traced: 103 us -> 101 us
  Pallas kernels: 101 us -> 99.6 us
    pallas_call x1, Pallas kernels: 101 us -> 99.6 us  [body(): pl.pallas_call(functools.partial(kernel, c, list(scratch)), out_shape=jax...]
where the time goes in v3:
time: 101 us
  Pallas kernels  99.6 us (99%)
  local copies, waits for them, and re-layouts  1.62 us (2%)
    pallas_call x1, Pallas kernels, body(): pl.pallas_call(functools.partial(kernel, c, list(scratch)), out_shape=jax...  99.6 us

profile of v3, /device:TPU:2, one launch (start us, length us, event | category | flops | bytes accessed | tf_op | source)
XLA Modules:
  0.0 101.2 jit_solution(6399258704526021875)
XLA Ops:
  0.0 99.6 %shard_map.109 = bf16[256,384]{1,0:T(8,128)(2,1)} custom-call(bf16[256,512]{1,0:T(8,128)(2,1)} %refs_0_.1, bf16[256,512]{1,0:T(8,128)(2,1)} %refs_1_.1, bf16[256,512]{1,0:T(8,128)(2,1)} %refs_2_.1, f32[4,256]{1,0:T(4,128)} %refs_3_.1, bf16[256,384]{1,0:T(8,128)(2,1)} %refs_4_.1, f32[384]{0:T(512)} %refs_5_.1, s32[2,256]{1,0:T(2,128)} %bitcast.3, ...), custom_call_target="tpu_custom_call" | custom-call | tf_op jit(solution)/shard_map/pallas_call | solution.py:648
  99.6 1.6 %copy.13 = bf16[256,384]{1,0:T(8,128)(2,1)} copy(bf16[256,384]{1,0:T(8,128)(2,1)} %shard_map.109) | data formatting | bytes 393216

commit v4 on v3

--- a/solution.py
+++ b/solution.py
@@ -200,7 +200,7 @@
 
         lax.fori_loop(1, tp_n, step, 0)
 
-    pending = []
+    pending, last_sent = [], []
     barrier = pltpu.get_barrier_semaphore()
     seq_peers(
         lambda p: pl.semaphore_signal(barrier, inc=1, device_id=(p, tp), device_id_type=MESH)
@@ -362,17 +362,20 @@
     home_slot = starts[home_group]
 
     def group_peers(g, sign, body):
-        def step(j, carry):
+        first = 0 if g != home_group else 1
+
+        def step(i, carry):
+            j = sizes[g] - 1 + first - i
             dz = groups[g][0]
-            for i in range(1, len(groups[g])):
-                dz = jnp.where(j < i * xs, dz, groups[g][i])
+            for chip in range(1, len(groups[g])):
+                dz = jnp.where(j < chip * xs, dz, groups[g][chip])
             dx = lax.rem(j, xs)
             pz = lax.rem(z + zs + sign * dz, zs)
             px = lax.rem(x + xs + sign * dx, xs)
             body(starts[g] + j, pz * xs + px)
             return carry
 
-        lax.fori_loop(0 if g != home_group else 1, sizes[g], step, 0)
+        lax.fori_loop(first, sizes[g], step, 0)
 
     for g in range(len(groups)):
         group_peers(
@@ -563,7 +566,7 @@
                 hs.at[:, rows_of(j)], ret.at[:, rows_of(s)], r["h_s"].at[g], m_r.at[5], (p, tp)
             ),
         )
-        pending.append((group_ref(g), r["h_s"].at[g]))
+        last_sent.append((group_ref(g), r["h_s"].at[g]))
         if g == home_group:
             ret[:, rows_of(s)] = hs[:, home_slot * TILE : (home_slot + 1) * TILE]
 
@@ -583,6 +586,8 @@
         gates.append(jax.nn.sigmoid(logit))
     both = gates[0] + gates[1]
     shares = [to_column(gate / both) for gate in gates]
+    for ref, sem in pending:
+        wait(ref, sem)
     wait(ret.at[:, pl.ds(0, (n - 1) * TILE)], m_r.at[5])
     mixed = hidden
     for j in range(2):
@@ -590,7 +595,7 @@
         mixed = mixed + shares[j] * from_pieces(parts, ret, pl.ds(0, n * TILE))
     out[...] = mixed.astype(BF16)
 
-    for ref, sem in pending:
+    for ref, sem in last_sent:
         wait(ref, sem)
 
 

time: 101 us -> 101 us (level)
  no operation moved by 1% of the time
where the time goes in v4:
time: 101 us
  Pallas kernels  99 us (98%)
  local copies, waits for them, and re-layouts  1.62 us (2%)
    pallas_call x1, Pallas kernels, body(): pl.pallas_call(functools.partial(kernel, c, list(scratch)), out_shape=jax...  99 us

profile of v4, /device:TPU:2, one launch (start us, length us, event | category | flops | bytes accessed | tf_op | source)
XLA Modules:
  0.0 100.6 jit_solution(14309539257754801950)
XLA Ops:
  0.0 99.0 %shard_map.109 = bf16[256,384]{1,0:T(8,128)(2,1)} custom-call(bf16[256,512]{1,0:T(8,128)(2,1)} %refs_0_.1, bf16[256,512]{1,0:T(8,128)(2,1)} %refs_1_.1, bf16[256,512]{1,0:T(8,128)(2,1)} %refs_2_.1, f32[4,256]{1,0:T(4,128)} %refs_3_.1, bf16[256,384]{1,0:T(8,128)(2,1)} %refs_4_.1, f32[384]{0:T(512)} %refs_5_.1, s32[2,256]{1,0:T(2,128)} %bitcast.3, ...), custom_call_target="tpu_custom_call" | custom-call | tf_op jit(solution)/shard_map/pallas_call | solution.py:653
  99.0 1.6 %copy.13 = bf16[256,384]{1,0:T(8,128)(2,1)} copy(bf16[256,384]{1,0:T(8,128)(2,1)} %shard_map.109) | data formatting | bytes 393216

commit v5 on v4

--- a/solution.py
+++ b/solution.py
@@ -282,6 +282,19 @@
     for i in range(3):
         r["pm"][i] = flag((place == targets[0][i]) | (place == targets[1][i]))
 
+    def compaction(count):
+        row, lane = iota((count * CAP, count * TILE), 0), iota((count * CAP, count * TILE), 1)
+        block = (row * 2731) >> 16
+        return [flag(lane == place) for place in places(block, row - block * CAP)]
+
+    def expansion(count):
+        row, lane = iota((count * TILE, count * CAP), 0), iota((count * TILE, count * CAP), 1)
+        block = (lane * 2731) >> 16
+        return [flag(row == place) for place in places(block, lane - block * CAP)]
+
+    pack_parts = {count: compaction(count) for count in sorted(set(sizes))}
+    spread_parts = {count: expansion(count) for count in sorted(set(sizes))}
+
     causal = iota((t, t), 0) >= iota((t, t), 1)
     for h in range(heads):
         head = pl.ds(h * 128, 128)
@@ -441,16 +454,6 @@
     xg, mb, ps, pr = (r[name] for name in ("xg", "mb", "ps", "pr"))
     ys, yr, rl, hs = (r[name] for name in ("ys", "yr", "rl", "hs"))
 
-    def compaction(count):
-        row, lane = iota((count * CAP, count * TILE), 0), iota((count * CAP, count * TILE), 1)
-        block = (row * 2731) >> 16
-        return [flag(lane == place) for place in places(block, row - block * CAP)]
-
-    def expansion(count):
-        row, lane = iota((count * TILE, count * CAP), 0), iota((count * TILE, count * CAP), 1)
-        block = (lane * 2731) >> 16
-        return [flag(row == place) for place in places(block, lane - block * CAP)]
-
     def slots_of(g, unit):
         return pl.ds(starts[g] * unit, sizes[g] * unit)
 
@@ -464,7 +467,7 @@
 
     def spread_out(g):
         wait(group_ref(g), r["x_r"].at[g])
-        packed = from_pieces(compaction(sizes[g]), xr, slots_of(g, TILE)).astype(BF16)
+        packed = from_pieces(pack_parts[sizes[g]], xr, slots_of(g, TILE)).astype(BF16)
         xg[tp, rows_in(g)] = packed
         piece = xg.at[tp, rows_in(g)]
         for i, (_, device) in enumerate(sides):
@@ -558,7 +561,7 @@
             wait(yr.at[i, half_rows(g, 1 - i)], r["e_r"].at[g, i])
             wait(yr.at[i, half_rows(g, i)], r["d_r"].at[g, i])
             total = total + yr[i, rows_in(g)].astype(F32)
-        to_pieces(expansion(sizes[g]), total.astype(BF16), hs, slots_of(g, TILE))
+        to_pieces(spread_parts[sizes[g]], total.astype(BF16), hs, slots_of(g, TILE))
         group_peers(
             g,
             -1,

time: 101 us -> 101 us (level)
  no operation moved by 1% of the time
where the time goes in v5:
time: 101 us
  Pallas kernels  99 us (98%)
  local copies, waits for them, and re-layouts  1.62 us (2%)
    pallas_call x1, Pallas kernels, body(): pl.pallas_call(functools.partial(kernel, c, list(scratch)), out_shape=jax...  99 us

profile of v5, /device:TPU:2, one launch (start us, length us, event | category | flops | bytes accessed | tf_op | source)
XLA Modules:
  0.0 100.6 jit_solution(16179975000522102648)
XLA Ops:
  0.0 99.0 %shard_map.109 = bf16[256,384]{1,0:T(8,128)(2,1)} custom-call(bf16[256,512]{1,0:T(8,128)(2,1)} %refs_0_.1, bf16[256,512]{1,0:T(8,128)(2,1)} %refs_1_.1, bf16[256,512]{1,0:T(8,128)(2,1)} %refs_2_.1, f32[4,256]{1,0:T(4,128)} %refs_3_.1, bf16[256,384]{1,0:T(8,128)(2,1)} %refs_4_.1, f32[384]{0:T(512)} %refs_5_.1, s32[2,256]{1,0:T(2,128)} %bitcast.3, ...), custom_call_target="tpu_custom_call" | custom-call | tf_op jit(solution)/shard_map/pallas_call | solution.py:656
  99.0 1.6 %copy.13 = bf16[256,384]{1,0:T(8,128)(2,1)} copy(bf16[256,384]{1,0:T(8,128)(2,1)} %shard_map.109) | data formatting | bytes 393216
